TPU v7x, 32 devices: a whole 2x2x4 slice. The times are simulated.
32 devices in a mesh: patch: 8 (over z, x), tile: 4 (over y, core).
Axes of the slice: x: 2, y: 2, z: 4, core: 2. Of those that a mesh axis runs over, the one named last changes fastest.
Arguments:
- latents: float32 [1088, 128], P('patch')
- timestamps: int32 [1088], P('patch'), may hold values from 0 to 56, as said below
- cell_map: int32 [1024], replicated, may hold values from 0 to 1023, as said below
- w_video: bfloat16 [128, 3072], replicated, may hold values from -0.5 to 0.5
- w_audio: bfloat16 [128, 3072], replicated, may hold values from -0.5 to 0.5
- mod_scale: float32 [2, 3072], replicated, may hold values from -3 to 3
- mod_shift: float32 [2, 3072], replicated, may hold values from -3 to 3
- w_query: bfloat16 [3072, 3072], P(None, 'tile')
- w_key: bfloat16 [3072, 3072], P(None, 'tile')
- w_value: bfloat16 [3072, 3072], P(None, 'tile'), may hold values from -0.109375 to 0.109375
- q_gain: float32 [3072], P('tile'), as said below
- k_gain: float32 [3072], P('tile'), as said below
- k_cache: bfloat16 [1088, 3072], P('patch', 'tile'), may hold values from -8 to 8
- v_cache: bfloat16 [1088, 3072], P('patch', 'tile'), may hold values from -6 to 6
- w_out: bfloat16 [3072, 3072], P('tile'), may hold values from -0.109375 to 0.109375
- out_gain: float32 [3072], replicated, may hold values from 0.25 to 1.75
- w_final: bfloat16 [3072, 128], replicated, may hold values from -0.109375 to 0.109375
- step_sizes: float32 [2], replicated, may hold values from 0.2 to 0.6
- conv_w: bfloat16 [3, 3, 3, 128, 512], replicated, may hold values from -0.109375 to 0.109375
- conv_b: float32 [512], replicated, may hold values from -3 to 3
Outputs:
- final_latents: float32 [1088, 128], P('patch')
- decoded: bfloat16 [8, 16, 8, 512], P(None, 'patch', 'tile')
Inputs may be any that keep to these rules, and one draw needn't show every extreme that they name: `cell_map`: a permutation of the 1024 cells of the grid; entry r is the cell of the r-th video token, which stands in patch shard r // 128; cell (f, h, w) belongs to the decode block (h // 2, w // 2), held by patch index h // 2 and tile index w // 2; every patch shard holds exactly 4 cells of every decode block. A video token's timestamp is 8 times the frame of its cell; audio tokens' timestamps lie in the same span. `q_gain`: positive. `k_gain`: positive.
All inputs are finite; a program needn't handle non-finite values.
Results may differ from a plain program's by a relative error of at most 0.009.
Values may be sent and summed in bfloat16 or wider, within the bound.
A program may use at most 128 MiB of HBM per device.

v0:
```python
import functools

import jax
import jax.numpy as jnp
from jax import lax
from jax.experimental import pallas as pl
from jax.experimental.pallas import tpu as pltpu
from jax.sharding import PartitionSpec as P

HEAD = 128
VID_DEV = 128
STEPS = 2
FRAMES = 8
BH = 2
EPSILON = 1e-06
MESH = pl.DeviceIdType.MESH
F32 = jnp.float32
BF16 = jnp.bfloat16


def dot(a, b):
    return jnp.dot(a, b, preferred_element_type=F32)


def kernel(
    n,
    nt,
    latents,
    stamps,
    cells,
    mod_scale,
    mod_shift,
    q_gain,
    k_gain,
    k_cache,
    v_cache,
    out_gain,
    step_sizes,
    conv_b,
    wv_hbm,
    wa_hbm,
    wq_hbm,
    wk_hbm,
    wval_hbm,
    wo_hbm,
    wf_hbm,
    cw_hbm,
    state_out,
    conv_out,
    w_vid,
    w_aud,
    w_q,
    w_k,
    w_val,
    w_o,
    w_f,
    kv,
    emb,
    normed,
    q_ref,
    att,
    cos_ref,
    sin_ref,
    acc,
    s1_send,
    s1_recv,
    s2_send,
    s2_recv,
    vel_send,
    vel_recv,
    vid,
    onehot,
    grown,
    load_sem,
    ring_send,
    ring_recv,
    s1_ss,
    s1_rs,
    s2_ss,
    s2_rs,
    v_ss,
    v_rs,
    vid_ss,
    vid_rs,
):
    rows = latents.shape[0]
    pad = kv.shape[4]
    width = emb.shape[1]
    cols = q_ref.shape[1]
    half = cols // 2
    quarter = width // nt
    me = lax.axis_index("patch")
    tile = lax.axis_index("tile")
    core = tile % 2
    ty = tile // 2
    ny = nt // 2

    loads = []
    for i, (src, dst) in enumerate(
        (
            (wv_hbm, w_vid),
            (wa_hbm, w_aud),
            (wk_hbm, w_k),
            (wval_hbm, w_val),
            (wq_hbm, w_q),
            (wo_hbm, w_o),
            (wf_hbm, w_f),
        )
    ):
        copy = pltpu.make_async_copy(src, dst, load_sem.at[i])
        copy.start()
        loads.append(copy)

    barrier = pltpu.get_barrier_semaphore()
    for j in range(1, n):
        pl.semaphore_signal(
            barrier, inc=1, device_id=(lax.rem(me + j, n), tile), device_id_type=MESH
        )
    for j in range(1, nt):
        pl.semaphore_signal(
            barrier, inc=1, device_id=(me, lax.rem(tile + j, nt)), device_id_type=MESH
        )

    for d in range(2):
        for w, src in enumerate((k_cache, v_cache)):
            block = src[:, d * half : (d + 1) * half].astype(F32)
            block = jnp.concatenate([block, jnp.zeros((pad - rows, half), F32)], axis=0)
            kv[1, d, 0, w] = block.astype(BF16)
    pl.semaphore_wait(barrier, n - 1 + nt - 1)

    odd = me % 2
    pos = (1 - odd) * (me // 2) + odd * (n - 1 - me // 2)

    def at_pos(p):
        p = lax.rem(p + n, n)
        back = p // (n // 2)
        return (1 - back) * (2 * p) + back * (2 * (n - 1 - p) + 1)

    nexts = (at_pos(pos + 1), at_pos(pos - 1))

    def hop(step, s, w, d):
        if s > 0:
            src = kv.at[step, d, s, w]
        elif step == 0:
            src = kv.at[1, d, 0, w]
        else:
            src = kv.at[step - 1, d, 0, w]
        return pltpu.make_async_remote_copy(
            src_ref=src,
            dst_ref=kv.at[step, d, s + 1, w],
            send_sem=ring_send.at[step, d, s, w],
            recv_sem=ring_recv.at[step, d, s, w],
            device_id=(nexts[d], tile),
            device_id_type=MESH,
        )

    queue = [(step, s, w) for step in range(STEPS) for s in range(n - 1) for w in range(2)]
    done = [0]

    def start_hop(index):
        for d in range(2):
            hop(*queue[index], d).start()

    def service(limit=None):
        i = done[0]
        if i >= len(queue) or (limit is not None and queue[i][0] > limit):
            return
        for d in range(2):
            hop(*queue[i], d).wait_recv()
            if i + 2 < len(queue):
                hop(*queue[i + 2], d).start()
        done[0] = i + 1

    start_hop(0)
    start_hop(1)

    lane = lax.broadcasted_iota(jnp.int32, (1, HEAD), 1)
    frequency = jnp.exp(-jnp.log(F32(10000.0)) * (lane % (HEAD // 2)).astype(F32) / (HEAD // 2))
    here = lax.broadcasted_iota(jnp.int32, (rows, rows), 0)
    there = lax.broadcasted_iota(jnp.int32, (rows, rows), 1)
    times = jnp.where(here == there, stamps[...].astype(F32), 0.0)
    angles = jnp.sum(times, axis=1, keepdims=True) * frequency
    cos_ref[...] = jnp.cos(angles)
    sin_ref[...] = jnp.where(lane < HEAD // 2, -1.0, 1.0) * jnp.sin(angles)

    bw = VID_DEV // (nt * FRAMES * BH)
    gw = bw + 2
    slots = 2 * FRAMES
    row = lax.broadcasted_iota(jnp.int32, (onehot.shape[0], 1), 0)
    f_id = row % slots - 1
    h_id = row // (slots * gw) - 1 + me * BH
    w_id = row // slots % gw - 1 + tile * bw
    inside = (
        (f_id >= 0)
        & (f_id < FRAMES)
        & (h_id >= 0)
        & (h_id < n * BH)
        & (w_id >= 0)
        & (w_id < nt * bw)
    )
    wanted = jnp.where(inside, (f_id * (n * BH) + h_id) * (nt * bw) + w_id, -1)
    for j in range(n):
        c = slice(j * VID_DEV, (j + 1) * VID_DEV)
        onehot[:, c] = jnp.where(cells[:, c] == wanted, 1.0, 0.0).astype(BF16)

    state_out[...] = latents[...]
    waited = set()

    def need(i):
        if i not in waited:
            loads[i].wait()
            waited.add(i)

    chunk = 256

    def project(weight, gain, put):
        @pl.loop(0, cols // chunk)
        def _(i):
            cs = pl.ds(pl.multiple_of(i * chunk, chunk), chunk)
            raw = dot(normed[...], weight[:, cs])
            for h in range(chunk // HEAD):
                hs = pl.ds(pl.multiple_of(i * chunk + h * HEAD, HEAD), HEAD)
                x = raw[:, h * HEAD : (h + 1) * HEAD]
                if gain is not None:
                    x = x * lax.rsqrt(jnp.mean(x * x, axis=1, keepdims=True) + EPSILON)
                    x = x * gain[pl.ds(i * (chunk // HEAD) + h, 1), :]
                    x = x * cos_ref[...] + pltpu.roll(x, HEAD // 2, 1) * sin_ref[...]
                put(i * (chunk // HEAD) + h, hs, x)

    heads_half = half // HEAD

    for step in range(STEPS):
        need(0)
        need(1)
        state = state_out[...]
        vid_b = state[:VID_DEV].astype(BF16)
        aud_b = state[VID_DEV:].astype(BF16)
        square = jnp.zeros((rows, 1), F32)
        wide = width // 4
        for i in range(4):
            c = slice(i * wide, (i + 1) * wide)
            e = jnp.concatenate([dot(vid_b, w_vid[:, c]), dot(aud_b, w_aud[:, c])], axis=0)
            emb[:, c] = e
            square = square + jnp.sum(e * e, axis=1, keepdims=True)
        scale = lax.rsqrt(square / width + EPSILON)
        for i in range(4):
            c = slice(i * wide, (i + 1) * wide)
            x = emb[:, c] * scale * (1.0 + mod_scale[step : step + 1, c])
            normed[:, c] = (x + mod_shift[step : step + 1, c]).astype(BF16)
        service(step)
        service(step)

        def put_kv(which):
            def put(h, hs, x):
                x = jnp.concatenate([x, jnp.zeros((pad - rows, HEAD), F32)], axis=0)
                d = h // heads_half
                cs = pl.ds(pl.multiple_of((h % heads_half) * HEAD, HEAD), HEAD)
                kv[step, d, 0, which, :, cs] = x.astype(BF16)

            return put

        def put_q(h, hs, x):
            q_ref[:, hs] = x.astype(BF16)

        need(2)
        if step == 1:
            for d in range(2):
                for w in range(2):
                    hop(0, 0, w, d).wait_send()
        project(w_k, k_gain, put_kv(0))
        service(step)
        service(step)
        need(3)
        project(w_val, None, put_kv(1))
        service(step)
        service(step)
        need(4)
        project(w_q, q_gain, put_q)
        if step == STEPS - 1:
            taps = cw_hbm.shape[0]
            out_ch = cw_hbm.shape[1]
            conv_loads = [
                pltpu.make_async_copy(
                    cw_hbm.at[0:width], w_q.at[:, 0:out_ch], load_sem.at[7]
                ),
                pltpu.make_async_copy(
                    cw_hbm.at[width:taps], w_k.at[0 : taps - width, 0:out_ch], load_sem.at[8]
                ),
            ]
            for copy in conv_loads:
                copy.start()
        while done[0] < (step + 1) * 2 * (n - 1):
            service()

        for d in range(2):

            for h in range(heads_half):
                hs = slice(h * HEAD, (h + 1) * HEAD)
                qs = slice(d * half + h * HEAD, d * half + (h + 1) * HEAD)
                keys = kv[step, d, :, 0, :, hs].reshape(n * pad, HEAD)
                values = kv[step, d, :, 1, :, hs].reshape(n * pad, HEAD)
                scores = lax.dot_general(
                    q_ref[:, qs], keys, (((1,), (1,)), ((), ())), preferred_element_type=F32
                )
                key_id = lax.broadcasted_iota(jnp.int32, (1, n * pad), 1)
                scores = jnp.where(key_id % pad < rows, scores, -jnp.inf)
                top = jnp.max(scores, axis=1, keepdims=True)
                weights = jnp.exp((scores - top) * HEAD ** (-0.5))
                total = jnp.sum(weights, axis=1, keepdims=True)
                att[:, qs] = (dot(weights.astype(BF16), values) / total).astype(BF16)
                service()

        need(5)

        def out_part(owner):
            cs = pl.ds(pl.multiple_of(owner * quarter, HEAD), quarter)
            return dot(att[...], w_o[:, cs])

        def pad_rows(x):
            return jnp.concatenate([x, jnp.zeros((pad - rows, x.shape[1]), F32)], axis=0)

        def tile_copy(src, dst, ss, rs, target):
            return pltpu.make_async_remote_copy(
                src_ref=src,
                dst_ref=dst,
                send_sem=ss,
                recv_sem=rs,
                device_id=(me, target),
                device_id_type=MESH,
            )

        sibling = ty * 2 + 1 - core
        first = []
        for j in list(range(1, ny)) + [0]:
            chip = lax.rem(ty + j, ny)
            s1_send[j] = pad_rows(out_part(chip * 2 + 1 - core)).astype(BF16)
            copy = tile_copy(
                s1_send.at[j], s1_recv.at[j], s1_ss.at[step, j], s1_rs.at[step, j], sibling
            )
            copy.start()
            first.append((j, copy))
            service()
        second = []
        for j, copy in first:
            chip = lax.rem(ty + j, ny)
            mine = out_part(chip * 2 + core)
            service()
            copy.wait_recv()
            mine = mine + s1_recv[j].astype(F32)[:rows]
            if j > 0:
                s2_send[j - 1] = pad_rows(mine).astype(BF16)
                far = tile_copy(
                    s2_send.at[j - 1],
                    s2_recv.at[j - 1],
                    s2_ss.at[step, j],
                    s2_rs.at[step, j],
                    chip * 2 + core,
                )
                far.start()
                second.append((j, far))
            else:
                es = pl.ds(pl.multiple_of(tile * quarter, HEAD), quarter)
                acc[...] = mine + emb[:, es]
        service()
        for j, far in second:
            far.wait_recv()
            acc[...] += s2_recv[j - 1].astype(F32)[:rows]
        need(6)
        mixed = acc[...]
        es = pl.ds(pl.multiple_of(tile * quarter, HEAD), quarter)
        square = jnp.sum(mixed * mixed, axis=1, keepdims=True)
        part = dot((mixed * out_gain[:, es]).astype(BF16), w_f[es, :])
        vel_send[0] = jnp.concatenate(
            [part, jnp.broadcast_to(square, (rows, HEAD))], axis=1
        )
        near = tile_copy(
            vel_send.at[0], vel_recv.at[0], v_ss.at[step, 0], v_rs.at[step, 0], sibling
        )
        near.start()
        service()
        near.wait_recv()
        both = vel_send[0] + vel_recv[0]
        vel_send[1] = both
        others = []
        for j in range(1, ny):
            copy = tile_copy(
                vel_send.at[1],
                vel_recv.at[j],
                v_ss.at[step, j],
                v_rs.at[step, j],
                lax.rem(ty + j, ny) * 2 + core,
            )
            copy.start()
            others.append(copy)
        service()
        for j, copy in enumerate(others):
            copy.wait_recv()
            both = both + vel_recv[j + 1]
        channels = part.shape[1]
        scale = lax.rsqrt(both[:, channels : channels + 1] / width + EPSILON)
        state_out[...] = state - step_sizes[step] * (both[:, :channels] * scale)
        for _, copy in first:
            copy.wait_send()
        for _, copy in second:
            copy.wait_send()
        near.wait_send()
        for copy in others:
            copy.wait_send()

    vid[me] = state_out[:VID_DEV, :].astype(BF16)
    sends = []
    for j in list(range(1, n)):
        copy = pltpu.make_async_remote_copy(
            src_ref=vid.at[me],
            dst_ref=vid.at[me],
            send_sem=vid_ss.at[j],
            recv_sem=vid_rs.at[j],
            device_id=(lax.rem(me + j, n), tile),
            device_id_type=MESH,
        )
        copy.start()
        sends.append(copy)
    for index in range(2, len(queue)):
        for d in range(2):
            hop(*queue[index], d).wait_send()
    for copy in conv_loads:
        copy.wait()
    for j in range(1, n):
        source = lax.rem(me - j + n, n)
        pltpu.make_async_remote_copy(
            src_ref=vid.at[source],
            dst_ref=vid.at[source],
            send_sem=vid_ss.at[j],
            recv_sem=vid_rs.at[j],
            device_id=(source, tile),
            device_id_type=MESH,
        ).wait_recv()
    grown[...] = dot(onehot[...], vid[...].reshape(n * VID_DEV, HEAD))
    pieces = []
    for a in range(3):
        for b in range(3):
            for c in range(3):
                starts = [
                    ((h + b) * gw + w + c) * slots + a for h in range(BH) for w in range(bw)
                ]
                pieces.append(
                    jnp.concatenate([grown[s : s + FRAMES, :] for s in starts], axis=0).astype(BF16)
                )
    cut = width // HEAD
    total = dot(jnp.concatenate(pieces[:cut], axis=1), w_q[:, 0:out_ch])
    total = total + dot(jnp.concatenate(pieces[cut:], axis=1), w_k[0 : taps - width, 0:out_ch])
    conv_out[...] = (total + conv_b[...]).astype(BF16)
    for copy in sends:
        copy.wait_send()


def local(
    latents,
    timestamps,
    cell_map,
    w_video,
    w_audio,
    mod_scale,
    mod_shift,
    w_query,
    w_key,
    w_value,
    q_gain,
    k_gain,
    k_cache,
    v_cache,
    w_out,
    out_gain,
    w_final,
    step_sizes,
    conv_w,
    conv_b,
):
    n, nt = lax.axis_size("patch"), lax.axis_size("tile")
    rows, channels = latents.shape
    width = w_query.shape[0]
    cols = w_query.shape[1]
    pad = -(-rows // 16) * 16
    quarter = width // nt
    ny = nt // 2
    bw = VID_DEV // (nt * FRAMES * BH)
    border = (BH + 2) * (bw + 2) * 2 * FRAMES
    cells = FRAMES * BH * bw
    out_ch = conv_w.shape[-1]
    conv_flat = conv_w.reshape(-1, out_ch)
    vmem = pl.BlockSpec(memory_space=pltpu.VMEM)
    hbm = pl.BlockSpec(memory_space=pl.ANY)
    dma = pltpu.SemaphoreType.DMA
    state, conv = pl.pallas_call(
        functools.partial(kernel, n, nt),
        out_shape=(
            jax.ShapeDtypeStruct((rows, channels), F32),
            jax.ShapeDtypeStruct((cells, out_ch), BF16),
        ),
        in_specs=[vmem] * 10 + [pl.BlockSpec(memory_space=pltpu.SMEM), vmem] + [hbm] * 8,
        out_specs=(vmem, vmem),
        scratch_shapes=[
            pltpu.VMEM(w_video.shape, BF16),
            pltpu.VMEM(w_audio.shape, BF16),
            pltpu.VMEM(w_query.shape, BF16),
            pltpu.VMEM(w_key.shape, BF16),
            pltpu.VMEM(w_value.shape, BF16),
            pltpu.VMEM(w_out.shape, BF16),
            pltpu.VMEM(w_final.shape, BF16),
            pltpu.VMEM((STEPS, 2, n, 2, pad, cols // 2), BF16),
            pltpu.VMEM((rows, width), F32),
            pltpu.VMEM((rows, width), BF16),
            pltpu.VMEM((rows, cols), BF16),
            pltpu.VMEM((rows, cols), BF16),
            pltpu.VMEM((rows, HEAD), F32),
            pltpu.VMEM((rows, HEAD), F32),
            pltpu.VMEM((rows, quarter), F32),
            pltpu.VMEM((ny, pad, quarter), BF16),
            pltpu.VMEM((ny, pad, quarter), BF16),
            pltpu.VMEM((ny - 1, pad, quarter), BF16),
            pltpu.VMEM((ny - 1, pad, quarter), BF16),
            pltpu.VMEM((2, rows, channels + HEAD), F32),
            pltpu.VMEM((ny, rows, channels + HEAD), F32),
            pltpu.VMEM((n, VID_DEV, channels), BF16),
            pltpu.VMEM((border, n * VID_DEV), BF16),
            pltpu.VMEM((border, channels), F32),
            dma((9,)),
            dma((STEPS, 2, n - 1, 2)),
            dma((STEPS, 2, n - 1, 2)),
            dma((STEPS, ny)),
            dma((STEPS, ny)),
            dma((STEPS, ny)),
            dma((STEPS, ny)),
            dma((STEPS, ny)),
            dma((STEPS, ny)),
            dma((n,)),
            dma((n,)),
        ],
        compiler_params=pltpu.CompilerParams(
            collective_id=0, has_side_effects=True, vmem_limit_bytes=63 * 1024 * 1024
        ),
    )(
        latents,
        timestamps.reshape(1, -1),
        cell_map.reshape(1, -1),
        mod_scale,
        mod_shift,
        q_gain.reshape(-1, HEAD),
        k_gain.reshape(-1, HEAD),
        k_cache,
        v_cache,
        out_gain.reshape(1, -1),
        step_sizes,
        conv_b.reshape(1, -1),
        w_video,
        w_audio,
        w_query,
        w_key,
        w_value,
        w_out,
        w_final,
        conv_flat,
    )
    decoded = conv.reshape(BH, bw, FRAMES, out_ch).transpose(2, 0, 1, 3)
    return state, decoded


def solution(mesh):
    return jax.shard_map(
        local,
        mesh=mesh,
        in_specs=(
            P("patch", None),
            P("patch"),
            P(),
            P(),
            P(),
            P(),
            P(),
            P(None, "tile"),
            P(None, "tile"),
            P(None, "tile"),
            P("tile"),
            P("tile"),
            P("patch", "tile"),
            P("patch", "tile"),
            P("tile", None),
            P(),
            P(),
            P(),
            P(),
            P(),
        ),
        out_specs=(P("patch", None), P(None, "patch", "tile", None)),
        check_vma=False,
    )
```

profile of v0, /device:TPU:0, one launch (start us, length us, event | category | flops | bytes accessed | tf_op | source)
XLA Modules:
  0.0 112.8 jit_solution(8788970441785093094)
XLA Ops:
  0.6 109.3 %shard_map.203 = (f32[136,128]{1,0:T(8,128)}, bf16[32,512]{1,0:T(8,128)(2,1)}) custom-call(f32[136,128]{1,0:T(8,128)} %latents.1, s32[1,136]{1,0:T(1,128)} %bitcast.19, s32[1,1024]{1,0:T(1,128)} %bitcast.15, f32[2,3072]{1,0:T(2,128)} %mod_scale.1, f32[2,3072]{1,0:T(2,128)} %mod_shift.1, f32[6,128]{1,0:T(8,128)} %bitcast.16, f32[6,128]{1,0:T(8,128)} %bitcast.17, ...), custom_call_target="tpu_custom_call" | custom-call | tf_op jit(solution)/shard_map/pallas_call | solution.py:494
  109.9 1.4 %copy.24 = bf16[2,2,8,512]{3,1,0,2:T(2,128)(2,1)} copy(bf16[2,2,8,512]{3,2,1,0:T(8,128)(2,1)} %bitcast.13) | data formatting | bytes 65536 | tf_op jit(solution)/shard_map/reshape | solution.py:564
  111.3 1.5 %copy.26 = f32[136,128]{1,0:T(8,128)} copy(f32[136,128]{1,0:T(8,128)} %get-tuple-element.8) | data formatting | bytes 139264
where the time goes:
time: 113 us
  Pallas kernels  109 us (96%)
  local copies, waits for them, and re-layouts  2.92 us (3%)
    pallas_call x1, Pallas kernels, local(): pl.pallas_call(functools.partial(kernel, n, nt), out_shape=(jax.ShapeDtyp...  109 us

commit v1 on v0

v1 whole, which is shorter than its diff:
```python
import functools

import jax
import jax.numpy as jnp
from jax import lax
from jax.experimental import pallas as pl
from jax.experimental.pallas import tpu as pltpu
from jax.sharding import PartitionSpec as P

HEAD = 128
VID_DEV = 128
AUD_DEV = 8
STEPS = 2
FRAMES = 8
BH = 2
EPSILON = 1e-06
MESH = pl.DeviceIdType.MESH
F32 = jnp.float32
BF16 = jnp.bfloat16


def dot(a, b):
    return jnp.dot(a, b, preferred_element_type=F32)


def kernel(
    n,
    nt,
    latents,
    stamps,
    cells,
    mod_scale,
    mod_shift,
    q_gain,
    k_gain,
    k_cache,
    v_cache,
    out_gain,
    step_sizes,
    conv_b,
    wv_hbm,
    wa_hbm,
    wq_hbm,
    wk_hbm,
    wval_hbm,
    wo_hbm,
    wf_hbm,
    cw_hbm,
    state_out,
    conv_out,
    w_vid,
    w_aud,
    w_qkv,
    w_o,
    w_f,
    w_c,
    kv0,
    kv1,
    lat,
    emb,
    normed,
    embq,
    q_ref,
    cs_ref,
    pair_cs,
    table,
    att,
    o_send,
    p_send,
    p_recv,
    acc,
    s1_send,
    s1_recv,
    s2_send,
    s2_recv,
    vel_send,
    vel_recv,
    vid,
    onehot,
    grown,
    load_sem,
    lz_ss,
    lz_rs,
    lx_ss,
    lx_rs,
    kz_ss,
    kz_rs,
    kx_ss,
    kx_rs,
    o_ss,
    o_rs,
    p_ss,
    p_rs,
    s1_ss,
    s1_rs,
    s2_ss,
    s2_rs,
    v_ss,
    v_rs,
    vid_ss,
    vid_rs,
):
    rows = latents.shape[0]
    pad = kv0.shape[3]
    width = emb.shape[1]
    hw = w_qkv.shape[1] // 3
    nh = hw // HEAD
    quarter = width // nt
    nz = n // 2
    npz = nz // 2
    me = lax.axis_index("patch")
    tile = lax.axis_index("tile")
    core = tile % 2
    ty = tile // 2
    ny = nt // 2
    zz = me // 2
    xx = me % 2
    h = zz % 2
    mate = me + 2 - 4 * h

    def half_cols(a):
        return pl.ds(pl.multiple_of(a * hw, HEAD), hw)

    loads = []
    for i, (src, dst) in enumerate(
        (
            (wv_hbm, w_vid),
            (wa_hbm, w_aud),
            (wk_hbm.at[:, half_cols(h)], w_qkv.at[:, 0:hw]),
            (wval_hbm.at[:, half_cols(h)], w_qkv.at[:, hw : 2 * hw]),
            (wq_hbm.at[:, half_cols(h)], w_qkv.at[:, 2 * hw : 3 * hw]),
            (wo_hbm, w_o),
            (wf_hbm, w_f),
            (cw_hbm, w_c),
        )
    ):
        copy = pltpu.make_async_copy(src, dst, load_sem.at[i])
        copy.start()
        loads.append(copy)

    barrier = pltpu.get_barrier_semaphore()
    for j in range(1, n):
        pl.semaphore_signal(
            barrier, inc=1, device_id=(lax.rem(me + j, n), tile), device_id_type=MESH
        )
    for j in range(1, nt):
        pl.semaphore_signal(
            barrier, inc=1, device_id=(me, lax.rem(tile + j, nt)), device_id_type=MESH
        )

    def padded(x):
        return jnp.concatenate([x, jnp.zeros((pad - rows, x.shape[1]), F32)], axis=0)

    line_row = lax.broadcasted_iota(jnp.int32, (pad - rows, HEAD), 0)
    aud_stamps = jnp.concatenate(
        [stamps[:, VID_DEV:rows], jnp.zeros((1, HEAD - AUD_DEV), jnp.int32)], axis=1
    ).astype(F32)
    vid_stamps = stamps[:, 0:VID_DEV].astype(F32)
    tail = jnp.where(line_row == 0, vid_stamps, jnp.where(line_row == 1, aud_stamps, 0.0))
    lat[xx, zz] = jnp.concatenate([latents[...], tail], axis=0).astype(BF16)

    for i in range(nh):
        for w, cache in enumerate((k_cache, v_cache)):
            for a, slot in ((h, 1), (1 - h, n + 2 + zz)):
                cs = pl.ds(pl.multiple_of(a * hw + i * HEAD, HEAD), HEAD)
                kv0[slot, i, w] = padded(cache[:, cs].astype(F32)).astype(BF16)
    pl.semaphore_wait(barrier, n - 1 + nt - 1)

    def remote(src, dst, ss, rs, patch):
        return pltpu.make_async_remote_copy(
            src_ref=src,
            dst_ref=dst,
            send_sem=ss,
            recv_sem=rs,
            device_id=(patch, tile),
            device_id_type=MESH,
        )

    def inside_line(z):
        return (z >= 0) & (z < nz)

    def lat_send(di, d):
        step = 1 - 2 * di
        s = zz - step * (d - 1)
        copy = remote(
            lat.at[xx, s], lat.at[xx, s], lz_ss.at[di, d - 1], lz_rs.at[di, d - 1], me + 2 * step
        )
        return inside_line(s) & inside_line(zz + step), copy

    def lat_arrive(di, d):
        step = 1 - 2 * di
        s = zz - step * d
        copy = remote(
            lat.at[xx, s], lat.at[xx, s], lz_ss.at[di, d - 1], lz_rs.at[di, d - 1], me - 2 * step
        )
        return inside_line(s), s, copy

    def lat_cross(s, line):
        return remote(
            lat.at[line, s], lat.at[line, s], lx_ss.at[s], lx_rs.at[s], me + 1 - 2 * xx
        )

    def lat_event(d):
        for di in range(2):
            there, s, copy = lat_arrive(di, d)

            @pl.when(there)
            def _():
                copy.wait_recv()
                if d + 1 < nz:
                    onward, forward = lat_send(di, d + 1)

                    @pl.when(onward)
                    def _():
                        forward.start()

                lat_cross(s, xx).start()

    def slot_of(z, s, a):
        other = 2 * lax.rem(s // 2 - z // 2 + npz, npz) + s % 2
        slot = jnp.where(s == z, 1, jnp.where(s == z + 1 - 2 * (z % 2), n, other))
        return jnp.where(a == z % 2, slot, n + 2 + s)

    def half_of(di, kind):
        return (1 - di) + kind * (2 * di - 1)

    def wanted_at(di, kind, z):
        return (kind == 0) | (z != (nz - 1 if di == 0 else 0))

    def kv_send(di, d, kind, i):
        step = 1 - 2 * di
        s = zz - step * (d - 1)
        a = half_of(di, kind)
        copy = remote(
            kv0.at[slot_of(zz, s, a), i],
            kv0.at[slot_of(zz + step, s, a), i],
            kz_ss.at[di, d - 1, kind, i],
            kz_rs.at[di, d - 1, kind, i],
            me + 2 * step,
        )
        return inside_line(s) & inside_line(zz + step) & wanted_at(di, kind, zz + step), copy

    def kv_cross(s, i, slot):
        return remote(
            kv0.at[slot, i], kv0.at[nz + s, i], kx_ss.at[s, i], kx_rs.at[s, i], me + 1 - 2 * xx
        )

    def event(e):
        d = e // (2 * nh) + 1
        kind = e // nh % 2
        i = e % nh
        for di in range(2):
            step = 1 - 2 * di
            s = zz - step * d
            a = half_of(di, kind)
            slot = slot_of(zz, s, a)

            @pl.when(inside_line(s) & wanted_at(di, kind, zz))
            def _():
                remote(
                    kv0.at[slot, i],
                    kv0.at[slot, i],
                    kz_ss.at[di, d - 1, kind, i],
                    kz_rs.at[di, d - 1, kind, i],
                    me - 2 * step,
                ).wait_recv()
                onward, forward = kv_send(di, d + 1, kind, i)

                @pl.when(onward)
                def _():
                    forward.start()

                @pl.when(a == h)
                def _():
                    kv_cross(s, i, slot).start()

    def start_own(kind, pieces):
        for i in pieces:
            for di in range(2):
                go, copy = kv_send(di, 1, kind, i)

                @pl.when(go)
                def _():
                    copy.start()

    for di in range(2):
        go, copy = lat_send(di, 1)

        @pl.when(go)
        def _():
            copy.start()

    lat_cross(zz, xx).start()
    start_own(0, (0,))
    kv_cross(zz, 0, 1).start()

    lane = lax.broadcasted_iota(jnp.int32, (1, HEAD), 1)
    frequency = jnp.exp(-jnp.log(F32(10000.0)) * (lane % (HEAD // 2)).astype(F32) / (HEAD // 2))
    times = lax.broadcasted_iota(jnp.int32, (HEAD // 2, HEAD), 0).astype(F32)
    angles = times * frequency
    waves = (jnp.cos(angles), jnp.where(lane < HEAD // 2, -1.0, 1.0) * jnp.sin(angles))
    for k, wave in enumerate(waves):
        top = wave.astype(BF16)
        cs = slice(k * HEAD, (k + 1) * HEAD)
        table[0 : HEAD // 2, cs] = top
        table[HEAD // 2 : HEAD, cs] = (wave - top.astype(F32)).astype(BF16)

    waited = set()

    def need(i):
        if i not in waited:
            loads[i].wait()
            waited.add(i)

    def embed(blocks, step):
        count = len(blocks)
        size = count * rows
        vid_b = jnp.concatenate([b[:VID_DEV] for b in blocks], axis=0).astype(BF16)
        aud_b = jnp.concatenate([b[VID_DEV:rows] for b in blocks], axis=0).astype(BF16)
        square = jnp.zeros((size, 1), F32)
        wide = width // 4
        for i in range(4):
            c = slice(i * wide, (i + 1) * wide)
            e = jnp.concatenate([dot(vid_b, w_vid[:, c]), dot(aud_b, w_aud[:, c])], axis=0)
            emb[0:size, c] = e
            square = square + jnp.sum(e * e, axis=1, keepdims=True)
        scale = lax.rsqrt(square / width + EPSILON)
        for i in range(4):
            c = slice(i * wide, (i + 1) * wide)
            x = emb[0:size, c] * scale * (1.0 + mod_scale[step : step + 1, c])
            normed[0:size, c] = (x + mod_shift[step : step + 1, c]).astype(BF16)

    def shard_rows(x, g, count):
        if count == 1:
            return x
        first = count * VID_DEV + g * AUD_DEV
        return jnp.concatenate(
            [x[g * VID_DEV : (g + 1) * VID_DEV], x[first : first + AUD_DEV]], axis=0
        )

    def rotate(x, gain, cos, sin):
        x = x * lax.rsqrt(jnp.mean(x * x, axis=1, keepdims=True) + EPSILON)
        x = x * gain
        return x * cos + pltpu.roll(x, HEAD // 2, 1) * sin

    def gain_row(gain, i):
        return gain[pl.ds(h * nh + i, 1), :]

    def project_kv(count, cos, sin, put):
        raw = dot(normed[0 : count * rows, :], w_qkv[:, 0 : 2 * hw])
        for i in range(nh):
            k = rotate(raw[:, i * HEAD : (i + 1) * HEAD], gain_row(k_gain, i), cos, sin)
            v = raw[:, hw + i * HEAD : hw + (i + 1) * HEAD]
            for g in range(count):
                for w, x in enumerate((k, v)):
                    put(g, i, w, padded(shard_rows(x, g, count)).astype(BF16))

    def project_q(count, cos, sin, targets):
        raw = dot(normed[0 : count * rows, :], w_qkv[:, 2 * hw : 3 * hw])
        for i in range(nh):
            q = rotate(raw[:, i * HEAD : (i + 1) * HEAD], gain_row(q_gain, i), cos, sin)
            for g in range(count):
                q_ref[targets[g], i] = padded(shard_rows(q, g, count)).astype(BF16)

    spot = lax.broadcasted_iota(jnp.int32, (HEAD, 3 * HEAD), 0) % (HEAD // 2)

    def pair_waves(blocks):
        aud = jnp.where(
            lane < AUD_DEV,
            blocks[0][rows + 1 : rows + 2],
            pltpu.roll(blocks[1][rows + 1 : rows + 2], AUD_DEV, 1),
        )
        line = jnp.concatenate([b[rows : rows + 1] for b in blocks] + [aud], axis=1)
        chosen = jnp.where(spot == line.astype(jnp.int32), 1.0, 0.0).astype(BF16)
        both = lax.dot_general(
            chosen, table[...], (((0,), (0,)), ((), ())), preferred_element_type=F32
        )
        pair_cs[0] = both[0 : 2 * rows, 0:HEAD]
        pair_cs[1] = both[0 : 2 * rows, HEAD : 2 * HEAD]

    bw = VID_DEV // (nt * FRAMES * BH)
    gw = bw + 2
    slots = 2 * FRAMES
    row = lax.broadcasted_iota(jnp.int32, (onehot.shape[0], 1), 0)
    f_id = row % slots - 1
    h_id = row // (slots * gw) - 1 + me * BH
    w_id = row // slots % gw - 1 + tile * bw
    inside = (
        (f_id >= 0)
        & (f_id < FRAMES)
        & (h_id >= 0)
        & (h_id < n * BH)
        & (w_id >= 0)
        & (w_id < nt * bw)
    )
    wanted = jnp.where(inside, (f_id * (n * BH) + h_id) * (nt * bw) + w_id, -1)
    for j in range(n):
        c = slice(j * VID_DEV, (j + 1) * VID_DEV)
        onehot[:, c] = jnp.where(cells[:, c] == wanted, 1.0, 0.0).astype(BF16)
    state_out[...] = latents[...]

    lat_event(1)
    start_own(0, range(1, nh))
    for i in range(1, nh):
        kv_cross(zz, i, 1).start()

    own_blocks = [lat[xx, zz].astype(F32), lat[xx, zz + 1 - 2 * h].astype(F32)]
    es = pl.ds(pl.multiple_of(tile * quarter, HEAD), quarter)
    need(0)
    need(1)
    embed(own_blocks, 0)
    embq[...] = padded(
        jnp.concatenate(
            [emb[0:VID_DEV, es], emb[2 * VID_DEV : 2 * VID_DEV + AUD_DEV, es]], axis=0
        )
    )
    if nz > 2:
        lat_event(2)
    start_own(1, range(nh))
    pair_waves(own_blocks)
    for g in range(2):
        for k in range(2):
            cs_ref[g, k] = shard_rows(pair_cs[k], g, 2)

    def put_own(g, i, w, x):
        if g == 0:
            kv0[n + 1, i, w] = x
            kv1[1, i, w] = x
        else:
            kv0[0, i, w] = x
            kv1[n, i, w] = x

    need(2)
    need(3)
    project_kv(2, pair_cs[0], pair_cs[1], put_own)
    for d in range(3, nz):
        lat_event(d)
    need(4)
    project_q(2, pair_cs[0], pair_cs[1], (0, 1))
    for e in range(nh):
        event(e)

    pairs = n // 2
    total_events = (nz - 1) * 2 * nh
    each = -(-(total_events - nh) // (pairs - 1))

    @pl.loop(1, pairs)
    def _(j):
        line = j % 2
        turn = j // 2
        first = 2 * lax.rem(zz // 2 + turn, npz)
        side = jnp.where(line == 0, xx, 1 - xx)

        @pl.when(line == 1)
        def _():
            for g in range(2):
                lat_cross(first + g, 1 - xx).wait_recv()

        blocks = [lat[side, first + g].astype(F32) for g in range(2)]
        embed(blocks, 0)
        base = nh + (j - 1) * each
        for e in range(each // 2):
            event(base + e)
        pair_waves(blocks)
        slot = jnp.where(line == 1, nz + first, 2 * turn)

        def put(g, i, w, x):
            kv1[slot + g, i, w] = x

        project_kv(2, pair_cs[0], pair_cs[1], put)
        for e in range(each // 2, each):
            event(base + e)

    def attend(keys_of, r, first, i):
        keys = keys_of[first : first + n, i, 0].reshape(n * pad, HEAD)
        values = keys_of[first : first + n, i, 1].reshape(n * pad, HEAD)
        scores = lax.dot_general(
            q_ref[r, i], keys, (((1,), (1,)), ((), ())), preferred_element_type=F32
        )
        key_id = lax.broadcasted_iota(jnp.int32, (1, n * pad), 1)
        scores = jnp.where(key_id % pad < rows, scores, -jnp.inf)
        top = jnp.max(scores, axis=1, keepdims=True)
        weights = jnp.exp((scores - top) * HEAD ** (-0.5))
        total = jnp.sum(weights, axis=1, keepdims=True)
        return (dot(weights.astype(BF16), values) / total).astype(BF16)

    for step in range(STEPS):
        state = state_out[...]
        if step > 0:

            def put_fresh(g, i, w, x):
                kv1[n + 1, i, w] = x

            def put_mate(g, i, w, x):
                kv1[0, i, w] = x

            embed([state], step)
            embq[...] = padded(emb[0:rows, es])
            project_kv(1, cs_ref[0, 0], cs_ref[0, 1], put_fresh)
            project_q(1, cs_ref[0, 0], cs_ref[0, 1], (0,))
            remote(p_send, p_recv, p_ss, p_rs, mate).wait_recv()
            embed([p_recv[...].astype(F32)], step)
            project_kv(1, cs_ref[1, 0], cs_ref[1, 1], put_mate)
            project_q(1, cs_ref[1, 0], cs_ref[1, 1], (1,))
        keys_of = kv0 if step == 0 else kv1
        swaps = []
        for i in range(nh):
            if step == 0:
                for s in range(nz):
                    kv_cross(s, i, nz + s).wait_recv()
            o_send[step, i] = attend(keys_of, 1, 0, i)
            copy = remote(
                o_send.at[step, i],
                att.at[step, h, i],
                o_ss.at[step, i],
                o_rs.at[step, i],
                mate,
            )
            copy.start()
            swaps.append(copy)
        for i in range(nh):
            att[step, h, i] = attend(keys_of, 0, 2, i)
        need(5)
        for i in range(nh):
            remote(
                o_send.at[step, i],
                att.at[step, 1 - h, i],
                o_ss.at[step, i],
                o_rs.at[step, i],
                mate,
            ).wait_recv()

        def out_part(owner):
            cs = pl.ds(pl.multiple_of(owner * quarter, HEAD), quarter)
            heads = [att[step, a, i] for a in range(2) for i in range(nh)]
            return dot(jnp.concatenate(heads, axis=1), w_o[:, cs])

        def tile_copy(src, dst, ss, rs, target):
            return pltpu.make_async_remote_copy(
                src_ref=src,
                dst_ref=dst,
                send_sem=ss,
                recv_sem=rs,
                device_id=(me, target),
                device_id_type=MESH,
            )

        sibling = ty * 2 + 1 - core
        first = []
        for j in list(range(1, ny)) + [0]:
            chip = lax.rem(ty + j, ny)
            s1_send[j] = out_part(chip * 2 + 1 - core).astype(BF16)
            copy = tile_copy(
                s1_send.at[j], s1_recv.at[j], s1_ss.at[step, j], s1_rs.at[step, j], sibling
            )
            copy.start()
            first.append((j, copy))
        second = []
        for j, copy in first:
            chip = lax.rem(ty + j, ny)
            mine = out_part(chip * 2 + core)
            copy.wait_recv()
            mine = mine + s1_recv[j].astype(F32)
            if j > 0:
                s2_send[j - 1] = mine.astype(BF16)
                far = tile_copy(
                    s2_send.at[j - 1],
                    s2_recv.at[j - 1],
                    s2_ss.at[step, j],
                    s2_rs.at[step, j],
                    chip * 2 + core,
                )
                far.start()
                second.append((j, far))
            else:
                acc[...] = mine + embq[...]
        for j, far in second:
            far.wait_recv()
            acc[...] += s2_recv[j - 1].astype(F32)
        need(6)
        mixed = acc[0:rows, :]
        square = jnp.sum(mixed * mixed, axis=1, keepdims=True)
        part = dot((mixed * out_gain[:, es]).astype(BF16), w_f[es, :])
        vel_send[0] = jnp.concatenate([part, jnp.broadcast_to(square, (rows, HEAD))], axis=1)
        near = tile_copy(
            vel_send.at[0], vel_recv.at[0], v_ss.at[step, 0], v_rs.at[step, 0], sibling
        )
        near.start()
        near.wait_recv()
        both = vel_send[0] + vel_recv[0]
        vel_send[1] = both
        others = []
        for j in range(1, ny):
            copy = tile_copy(
                vel_send.at[1],
                vel_recv.at[j],
                v_ss.at[step, j],
                v_rs.at[step, j],
                lax.rem(ty + j, ny) * 2 + core,
            )
            copy.start()
            others.append(copy)
        for j, copy in enumerate(others):
            copy.wait_recv()
            both = both + vel_recv[j + 1]
        channels = part.shape[1]
        scale = lax.rsqrt(both[:, channels : channels + 1] / width + EPSILON)
        new_state = state - step_sizes[step] * (both[:, :channels] * scale)
        state_out[...] = new_state
        if step < STEPS - 1:
            p_send[...] = padded(new_state).astype(BF16)
            remote(p_send, p_recv, p_ss, p_rs, mate).start()
        for _, copy in first:
            copy.wait_send()
        for _, copy in second:
            copy.wait_send()
        near.wait_send()
        for copy in others:
            copy.wait_send()
        for copy in swaps:
            copy.wait_send()

    vid[me] = state_out[:VID_DEV, :].astype(BF16)
    sends = []
    for j in list(range(1, n)):
        copy = remote(vid.at[me], vid.at[me], vid_ss.at[j], vid_rs.at[j], lax.rem(me + j, n))
        copy.start()
        sends.append(copy)

    remote(p_send, p_recv, p_ss, p_rs, mate).wait_send()
    for di in range(2):
        for d in range(1, nz):
            go, copy = lat_send(di, d)

            @pl.when(go)
            def _():
                copy.wait_send()

    for s in range(nz):
        lat_cross(s, xx).wait_send()
        for i in range(nh):
            kv_cross(s, i, 1).wait_send()

    @pl.loop(0, total_events)
    def _(e):
        for di in range(2):
            go, copy = kv_send(di, e // (2 * nh) + 1, e // nh % 2, e % nh)

            @pl.when(go)
            def _():
                copy.wait_send()

    need(7)
    for j in range(1, n):
        source = lax.rem(me - j + n, n)
        remote(vid.at[source], vid.at[source], vid_ss.at[j], vid_rs.at[j], source).wait_recv()
    grown[...] = dot(onehot[...], vid[...].reshape(n * VID_DEV, HEAD))
    pieces = []
    for a in range(3):
        for b in range(3):
            for c in range(3):
                starts = [
                    ((h_off + b) * gw + w + c) * slots + a
                    for h_off in range(BH)
                    for w in range(bw)
                ]
                pieces.append(
                    jnp.concatenate([grown[s : s + FRAMES, :] for s in starts], axis=0).astype(BF16)
                )
    total = dot(jnp.concatenate(pieces, axis=1), w_c[...])
    conv_out[...] = (total + conv_b[...]).astype(BF16)
    for copy in sends:
        copy.wait_send()


def local(
    latents,
    timestamps,
    cell_map,
    w_video,
    w_audio,
    mod_scale,
    mod_shift,
    w_query,
    w_key,
    w_value,
    q_gain,
    k_gain,
    k_cache,
    v_cache,
    w_out,
    out_gain,
    w_final,
    step_sizes,
    conv_w,
    conv_b,
):
    n, nt = lax.axis_size("patch"), lax.axis_size("tile")
    rows, channels = latents.shape
    width = w_query.shape[0]
    cols = w_query.shape[1]
    pad = -(-rows // 16) * 16
    quarter = width // nt
    ny = nt // 2
    nz = n // 2
    hw = cols // 2
    nh = hw // HEAD
    bw = VID_DEV // (nt * FRAMES * BH)
    border = (BH + 2) * (bw + 2) * 2 * FRAMES
    cells = FRAMES * BH * bw
    out_ch = conv_w.shape[-1]
    conv_flat = conv_w.reshape(-1, out_ch)
    vmem = pl.BlockSpec(memory_space=pltpu.VMEM)
    hbm = pl.BlockSpec(memory_space=pl.ANY)
    dma = pltpu.SemaphoreType.DMA
    state, conv = pl.pallas_call(
        functools.partial(kernel, n, nt),
        out_shape=(
            jax.ShapeDtypeStruct((rows, channels), F32),
            jax.ShapeDtypeStruct((cells, out_ch), BF16),
        ),
        in_specs=[vmem] * 10 + [pl.BlockSpec(memory_space=pltpu.SMEM), vmem] + [hbm] * 8,
        out_specs=(vmem, vmem),
        scratch_shapes=[
            pltpu.VMEM(w_video.shape, BF16),
            pltpu.VMEM(w_audio.shape, BF16),
            pltpu.VMEM((width, 3 * hw), BF16),
            pltpu.VMEM(w_out.shape, BF16),
            pltpu.VMEM(w_final.shape, BF16),
            pltpu.VMEM(conv_flat.shape, BF16),
            pltpu.VMEM((n + 2 + nz, nh, 2, pad, HEAD), BF16),
            pltpu.VMEM((n + 2, nh, 2, pad, HEAD), BF16),
            pltpu.VMEM((2, nz, pad, HEAD), BF16),
            pltpu.VMEM((2 * rows, width), F32),
            pltpu.VMEM((2 * rows, width), BF16),
            pltpu.VMEM((pad, quarter), F32),
            pltpu.VMEM((2, nh, pad, HEAD), BF16),
            pltpu.VMEM((2, 2, rows, HEAD), F32),
            pltpu.VMEM((2, 2 * rows, HEAD), F32),
            pltpu.VMEM((HEAD, 2 * HEAD), BF16),
            pltpu.VMEM((STEPS, 2, nh, pad, HEAD), BF16),
            pltpu.VMEM((STEPS, nh, pad, HEAD), BF16),
            pltpu.VMEM((pad, HEAD), BF16),
            pltpu.VMEM((pad, HEAD), BF16),
            pltpu.VMEM((pad, quarter), F32),
            pltpu.VMEM((ny, pad, quarter), BF16),
            pltpu.VMEM((ny, pad, quarter), BF16),
            pltpu.VMEM((ny - 1, pad, quarter), BF16),
            pltpu.VMEM((ny - 1, pad, quarter), BF16),
            pltpu.VMEM((2, rows, channels + HEAD), F32),
            pltpu.VMEM((ny, rows, channels + HEAD), F32),
            pltpu.VMEM((n, VID_DEV, channels), BF16),
            pltpu.VMEM((border, n * VID_DEV), BF16),
            pltpu.VMEM((border, channels), F32),
            dma((8,)),
            dma((2, nz - 1)),
            dma((2, nz - 1)),
            dma((nz,)),
            dma((nz,)),
            dma((2, nz - 1, 2, nh)),
            dma((2, nz - 1, 2, nh)),
            dma((nz, nh)),
            dma((nz, nh)),
            dma((STEPS, nh)),
            dma((STEPS, nh)),
            dma(()),
            dma(()),
            dma((STEPS, ny)),
            dma((STEPS, ny)),
            dma((STEPS, ny)),
            dma((STEPS, ny)),
            dma((STEPS, ny)),
            dma((STEPS, ny)),
            dma((n,)),
            dma((n,)),
        ],
        compiler_params=pltpu.CompilerParams(
            collective_id=0, has_side_effects=True, vmem_limit_bytes=63 * 1024 * 1024
        ),
    )(
        latents,
        timestamps.reshape(1, -1),
        cell_map.reshape(1, -1),
        mod_scale,
        mod_shift,
        q_gain.reshape(-1, HEAD),
        k_gain.reshape(-1, HEAD),
        k_cache,
        v_cache,
        out_gain.reshape(1, -1),
        step_sizes,
        conv_b.reshape(1, -1),
        w_video,
        w_audio,
        w_query,
        w_key,
        w_value,
        w_out,
        w_final,
        conv_flat,
    )
    decoded = conv.reshape(BH, bw, FRAMES, out_ch).transpose(2, 0, 1, 3)
    return state, decoded


def solution(mesh):
    return jax.shard_map(
        local,
        mesh=mesh,
        in_specs=(
            P("patch", None),
            P("patch"),
            P(),
            P(),
            P(),
            P(),
            P(),
            P(None, "tile"),
            P(None, "tile"),
            P(None, "tile"),
            P("tile"),
            P("tile"),
            P("patch", "tile"),
            P("patch", "tile"),
            P("tile", None),
            P(),
            P(),
            P(),
            P(),
            P(),
        ),
        out_specs=(P("patch", None), P(None, "patch", "tile", None)),
        check_vma=False,
    )
```

time: 113 us -> 89.4 us (0.79)
  Pallas kernels: 109 us -> 85.6 us
    pallas_call x1, Pallas kernels: 109 us -> 85.6 us  [local(): pl.pallas_call(functools.partial(kernel, n, nt), out_shape=(jax.ShapeDtyp...]
where the time goes in v1:
time: 89.4 us; the launch traced here: 89.1 us
  Pallas kernels  85.6 us (96%)
  local copies, waits for them, and re-layouts  2.92 us (3%)
    pallas_call x1, Pallas kernels, local(): pl.pallas_call(functools.partial(kernel, n, nt), out_shape=(jax.ShapeDtyp...  85.6 us

profile of v1, /device:TPU:0, one launch (start us, length us, event | category | flops | bytes accessed | tf_op | source)
XLA Modules:
  0.0 89.1 jit_solution(4881574188778065519)
XLA Ops:
  0.6 85.6 %shard_map.203 = (f32[136,128]{1,0:T(8,128)}, bf16[32,512]{1,0:T(8,128)(2,1)}) custom-call(f32[136,128]{1,0:T(8,128)} %latents.1, s32[1,136]{1,0:T(1,128)} %bitcast.19, s32[1,1024]{1,0:T(1,128)} %bitcast.15, f32[2,3072]{1,0:T(2,128)} %mod_scale.1, f32[2,3072]{1,0:T(2,128)} %mod_shift.1, f32[6,128]{1,0:T(8,128)} %bitcast.16, f32[6,128]{1,0:T(8,128)} %bitcast.17, ...), custom_call_target="tpu_custom_call" | custom-call | tf_op jit(solution)/shard_map/pallas_call | solution.py:716
  86.2 1.4 %copy.24 = bf16[2,2,8,512]{3,1,0,2:T(2,128)(2,1)} copy(bf16[2,2,8,512]{3,2,1,0:T(8,128)(2,1)} %bitcast.13) | data formatting | bytes 65536 | tf_op jit(solution)/shard_map/reshape | solution.py:802
  87.6 1.5 %copy.26 = f32[136,128]{1,0:T(8,128)} copy(f32[136,128]{1,0:T(8,128)} %get-tuple-element.8) | data formatting | bytes 139264

commit v2 on v1

--- a/solution.py
+++ b/solution.py
@@ -68,6 +68,9 @@
     o_send,
     p_send,
     p_recv,
+    state_ref,
+    st_send,
+    st_recv,
     acc,
     s1_send,
     s1_recv,
@@ -76,7 +79,9 @@
     vel_send,
     vel_recv,
     vid,
-    onehot,
+    got,
+    sel,
+    place,
     grown,
     load_sem,
     lz_ss,
@@ -101,18 +106,20 @@
     vid_rs,
 ):
     rows = latents.shape[0]
-    pad = kv0.shape[3]
+    pad = lat.shape[2]
     width = emb.shape[1]
     hw = w_qkv.shape[1] // 3
     nh = hw // HEAD
-    quarter = width // nt
+    part_rows = pad // (nt // 2)
+    wing = width // 2
     nz = n // 2
     npz = nz // 2
     me = lax.axis_index("patch")
     tile = lax.axis_index("tile")
     core = tile % 2
     ty = tile // 2
-    ny = nt // 2
+    chunks = acc.shape[0]
+    chunk = acc.shape[2]
     zz = me // 2
     xx = me % 2
     h = zz % 2
@@ -138,6 +145,7 @@
         copy.start()
         loads.append(copy)
 
+    got[...] = jnp.zeros(got.shape, BF16)
     barrier = pltpu.get_barrier_semaphore()
     for j in range(1, n):
         pl.semaphore_signal(
@@ -159,11 +167,16 @@
     tail = jnp.where(line_row == 0, vid_stamps, jnp.where(line_row == 1, aud_stamps, 0.0))
     lat[xx, zz] = jnp.concatenate([latents[...], tail], axis=0).astype(BF16)
 
+    def put_kv(where, slot, i, k, v):
+        where[slot, i, 0:VID_DEV] = k[:VID_DEV].astype(BF16)
+        where[slot, i, VID_DEV : 2 * VID_DEV] = v[:VID_DEV].astype(BF16)
+        last = jnp.concatenate([k[VID_DEV:], v[VID_DEV:]], axis=0)
+        where[slot, i, 2 * VID_DEV : 2 * rows] = last.astype(BF16)
+
     for i in range(nh):
-        for w, cache in enumerate((k_cache, v_cache)):
-            for a, slot in ((h, 1), (1 - h, n + 2 + zz)):
-                cs = pl.ds(pl.multiple_of(a * hw + i * HEAD, HEAD), HEAD)
-                kv0[slot, i, w] = padded(cache[:, cs].astype(F32)).astype(BF16)
+        for a, slot in ((h, 1), (1 - h, n + 2 + zz)):
+            cs = pl.ds(pl.multiple_of(a * hw + i * HEAD, HEAD), HEAD)
+            put_kv(kv0, slot, i, k_cache[:, cs].astype(F32), v_cache[:, cs].astype(F32))
     pl.semaphore_wait(barrier, n - 1 + nt - 1)
 
     def remote(src, dst, ss, rs, patch):
@@ -352,8 +365,7 @@
             k = rotate(raw[:, i * HEAD : (i + 1) * HEAD], gain_row(k_gain, i), cos, sin)
             v = raw[:, hw + i * HEAD : hw + (i + 1) * HEAD]
             for g in range(count):
-                for w, x in enumerate((k, v)):
-                    put(g, i, w, padded(shard_rows(x, g, count)).astype(BF16))
+                put(g, i, shard_rows(k, g, count), shard_rows(v, g, count))
 
     def project_q(count, cos, sin, targets):
         raw = dot(normed[0 : count * rows, :], w_qkv[:, 2 * hw : 3 * hw])
@@ -378,26 +390,7 @@
         pair_cs[0] = both[0 : 2 * rows, 0:HEAD]
         pair_cs[1] = both[0 : 2 * rows, HEAD : 2 * HEAD]
 
-    bw = VID_DEV // (nt * FRAMES * BH)
-    gw = bw + 2
-    slots = 2 * FRAMES
-    row = lax.broadcasted_iota(jnp.int32, (onehot.shape[0], 1), 0)
-    f_id = row % slots - 1
-    h_id = row // (slots * gw) - 1 + me * BH
-    w_id = row // slots % gw - 1 + tile * bw
-    inside = (
-        (f_id >= 0)
-        & (f_id < FRAMES)
-        & (h_id >= 0)
-        & (h_id < n * BH)
-        & (w_id >= 0)
-        & (w_id < nt * bw)
-    )
-    wanted = jnp.where(inside, (f_id * (n * BH) + h_id) * (nt * bw) + w_id, -1)
-    for j in range(n):
-        c = slice(j * VID_DEV, (j + 1) * VID_DEV)
-        onehot[:, c] = jnp.where(cells[:, c] == wanted, 1.0, 0.0).astype(BF16)
-    state_out[...] = latents[...]
+    state_ref[...] = padded(latents[...])
 
     lat_event(1)
     start_own(0, range(1, nh))
@@ -405,7 +398,7 @@
         kv_cross(zz, i, 1).start()
 
     own_blocks = [lat[xx, zz].astype(F32), lat[xx, zz + 1 - 2 * h].astype(F32)]
-    es = pl.ds(pl.multiple_of(tile * quarter, HEAD), quarter)
+    es = pl.ds(pl.multiple_of(core * wing, HEAD), wing)
     need(0)
     need(1)
     embed(own_blocks, 0)
@@ -422,13 +415,9 @@
         for k in range(2):
             cs_ref[g, k] = shard_rows(pair_cs[k], g, 2)
 
-    def put_own(g, i, w, x):
-        if g == 0:
-            kv0[n + 1, i, w] = x
-            kv1[1, i, w] = x
-        else:
-            kv0[0, i, w] = x
-            kv1[n, i, w] = x
+    def put_own(g, i, k, v):
+        put_kv(kv0, n + 1 if g == 0 else 0, i, k, v)
+        put_kv(kv1, 1 if g == 0 else n, i, k, v)
 
     need(2)
     need(3)
@@ -440,6 +429,64 @@
     for e in range(nh):
         event(e)
 
+    bw = VID_DEV // (nt * FRAMES * BH)
+    gw = bw + 2
+    slots = 2 * FRAMES
+    high, wide_w = n * BH, nt * bw
+    share = VID_DEV // (n * nt)
+    sent = sel.shape[1]
+    room = got.shape[1]
+    group = HEAD // room
+    row = lax.broadcasted_iota(jnp.int32, (place.shape[0], 1), 0)
+    f_id = row % slots - 1
+    h_id = row // (slots * gw) - 1 + me * BH
+    w_id = row // slots % gw - 1 + tile * bw
+    inside = (
+        (f_id >= 0)
+        & (f_id < FRAMES)
+        & (h_id >= 0)
+        & (h_id < high)
+        & (w_id >= 0)
+        & (w_id < wide_w)
+    )
+    wanted = jnp.where(inside, (f_id * high + h_id) * wide_w + w_id, -1)
+    down = lax.broadcasted_iota(jnp.int32, (VID_DEV, VID_DEV), 0)
+    along = lax.broadcasted_iota(jnp.int32, (VID_DEV, VID_DEV), 1)
+
+    def block_ranks(cell):
+        bh = cell // wide_w % high // BH
+        bc = cell % wide_w // bw
+        block = (bh * nt + bc).astype(F32)
+        column = jnp.sum(jnp.where(down == along, block, 0.0), axis=1, keepdims=True)
+        ahead = jnp.where((column == block) & (down < along), 1.0, 0.0)
+        return bh, bc, jnp.sum(ahead, axis=0, keepdims=True).astype(jnp.int32)
+
+    def slot_in(ranks, p):
+        bh, bc, rank = ranks
+        dh = bh - p + 1
+        dw = bc - tile + 1
+        near_by = (dh >= 0) & (dh < 3) & (dw >= 0) & (dw < 3)
+        return jnp.where(near_by, (dh * 3 + dw) * share + rank, -HEAD)
+
+    my_ranks = block_ranks(cells[:, pl.ds(pl.multiple_of(me * VID_DEV, VID_DEV), VID_DEV)])
+    pick = lax.broadcasted_iota(jnp.int32, (sent, VID_DEV), 0)
+    for j in range(n):
+        slot = slot_in(my_ranks, lax.rem(me + j, n))
+        sel[j] = jnp.where(pick == slot, 1.0, 0.0).astype(BF16)
+    for q in range(n // group):
+        found, moved = [], []
+        for k in range(group):
+            c = slice((q * group + k) * VID_DEV, (q * group + k + 1) * VID_DEV)
+            found.append(jnp.where(cells[:, c] == wanted, 1.0, 0.0).astype(BF16))
+            slot = slot_in(block_ranks(cells[:, c]), me) + k * room
+            moved.append(jnp.where(down == slot, 1.0, 0.0).astype(BF16))
+        place[:, q * HEAD : (q + 1) * HEAD] = lax.dot_general(
+            jnp.concatenate(found, axis=1),
+            jnp.concatenate(moved, axis=1),
+            (((1,), (1,)), ((), ())),
+            preferred_element_type=F32,
+        ).astype(BF16)
+
     pairs = n // 2
     total_events = (nz - 1) * 2 * nh
     each = -(-(total_events - nh) // (pairs - 1))
@@ -464,35 +511,42 @@
         pair_waves(blocks)
         slot = jnp.where(line == 1, nz + first, 2 * turn)
 
-        def put(g, i, w, x):
-            kv1[slot + g, i, w] = x
+        def put(g, i, k, v):
+            put_kv(kv1, slot + g, i, k, v)
 
         project_kv(2, pair_cs[0], pair_cs[1], put)
         for e in range(each // 2, each):
             event(base + e)
 
     def attend(keys_of, r, first, i):
-        keys = keys_of[first : first + n, i, 0].reshape(n * pad, HEAD)
-        values = keys_of[first : first + n, i, 1].reshape(n * pad, HEAD)
+        span = slice(first, first + n)
+        last = keys_of[span, i, 2 * VID_DEV : 2 * rows].astype(F32)
+        last_keys = last[:, :AUD_DEV].reshape(n * AUD_DEV, HEAD).astype(BF16)
+        last_values = last[:, AUD_DEV:].reshape(n * AUD_DEV, HEAD).astype(BF16)
+        keys = jnp.concatenate(
+            [keys_of[span, i, 0:VID_DEV].reshape(n * VID_DEV, HEAD), last_keys], axis=0
+        )
+        values = jnp.concatenate(
+            [keys_of[span, i, VID_DEV : 2 * VID_DEV].reshape(n * VID_DEV, HEAD), last_values],
+            axis=0,
+        )
         scores = lax.dot_general(
             q_ref[r, i], keys, (((1,), (1,)), ((), ())), preferred_element_type=F32
         )
-        key_id = lax.broadcasted_iota(jnp.int32, (1, n * pad), 1)
-        scores = jnp.where(key_id % pad < rows, scores, -jnp.inf)
         top = jnp.max(scores, axis=1, keepdims=True)
         weights = jnp.exp((scores - top) * HEAD ** (-0.5))
         total = jnp.sum(weights, axis=1, keepdims=True)
         return (dot(weights.astype(BF16), values) / total).astype(BF16)
 
     for step in range(STEPS):
-        state = state_out[...]
+        state = state_ref[...]
         if step > 0:
 
-            def put_fresh(g, i, w, x):
-                kv1[n + 1, i, w] = x
-
-            def put_mate(g, i, w, x):
-                kv1[0, i, w] = x
+            def put_fresh(g, i, k, v):
+                put_kv(kv1, n + 1, i, k, v)
+
+            def put_mate(g, i, k, v):
+                put_kv(kv1, 0, i, k, v)
 
             embed([state], step)
             embq[...] = padded(emb[0:rows, es])
@@ -530,10 +584,14 @@
                 mate,
             ).wait_recv()
 
-        def out_part(owner):
-            cs = pl.ds(pl.multiple_of(owner * quarter, HEAD), quarter)
-            heads = [att[step, a, i] for a in range(2) for i in range(nh)]
-            return dot(jnp.concatenate(heads, axis=1), w_o[:, cs])
+        heads = [att[step, a, i] for a in range(2) for i in range(nh)]
+        whole = jnp.concatenate(heads, axis=1).astype(F32)
+        turned = jnp.concatenate([whole[part_rows:], whole[:part_rows]], axis=0)
+        mine_att = jnp.where(ty == 0, turned, whole).astype(BF16)
+
+        def out_part(side, k):
+            cs = pl.ds(pl.multiple_of(side * wing + k * chunk, HEAD), chunk)
+            return dot(mine_att, w_o[:, cs])
 
         def tile_copy(src, dst, ss, rs, target):
             return pltpu.make_async_remote_copy(
@@ -546,86 +604,82 @@
             )
 
         sibling = ty * 2 + 1 - core
+        across = (1 - ty) * 2 + core
+        near_rows = pl.ds(pl.multiple_of(ty * part_rows, 8), part_rows)
         first = []
-        for j in list(range(1, ny)) + [0]:
-            chip = lax.rem(ty + j, ny)
-            s1_send[j] = out_part(chip * 2 + 1 - core).astype(BF16)
+        for k in range(chunks):
+            s1_send[k] = out_part(1 - core, k).astype(BF16)
             copy = tile_copy(
-                s1_send.at[j], s1_recv.at[j], s1_ss.at[step, j], s1_rs.at[step, j], sibling
+                s1_send.at[k], s1_recv.at[k], s1_ss.at[step, k], s1_rs.at[step, k], sibling
             )
             copy.start()
-            first.append((j, copy))
+            first.append(copy)
         second = []
-        for j, copy in first:
-            chip = lax.rem(ty + j, ny)
-            mine = out_part(chip * 2 + core)
-            copy.wait_recv()
-            mine = mine + s1_recv[j].astype(F32)
-            if j > 0:
-                s2_send[j - 1] = mine.astype(BF16)
+        far_parts = []
+        for k in range(chunks):
+            mine = out_part(core, k)
+            first[k].wait_recv()
+            mine = mine + s1_recv[k].astype(F32)
+            far_parts.append(mine[:part_rows])
+            ks = pl.ds(k * chunk, chunk)
+            acc[k] = mine[part_rows:] + embq[near_rows, ks]
+            if k % 2 == 1:
+                j = k // 2
+                s2_send[j] = jnp.concatenate(far_parts, axis=0).astype(BF16)
+                far_parts = []
                 far = tile_copy(
-                    s2_send.at[j - 1],
-                    s2_recv.at[j - 1],
-                    s2_ss.at[step, j],
-                    s2_rs.at[step, j],
-                    chip * 2 + core,
+                    s2_send.at[j], s2_recv.at[j], s2_ss.at[step, j], s2_rs.at[step, j], across
                 )
                 far.start()
-                second.append((j, far))
-            else:
-                acc[...] = mine + embq[...]
-        for j, far in second:
+                second.append(far)
+        need(6)
+        square = jnp.zeros((part_rows, 1), F32)
+        part = jnp.zeros((part_rows, w_f.shape[1]), F32)
+        for j, far in enumerate(second):
             far.wait_recv()
-            acc[...] += s2_recv[j - 1].astype(F32)
-        need(6)
-        mixed = acc[0:rows, :]
-        square = jnp.sum(mixed * mixed, axis=1, keepdims=True)
-        part = dot((mixed * out_gain[:, es]).astype(BF16), w_f[es, :])
-        vel_send[0] = jnp.concatenate([part, jnp.broadcast_to(square, (rows, HEAD))], axis=1)
-        near = tile_copy(
-            vel_send.at[0], vel_recv.at[0], v_ss.at[step, 0], v_rs.at[step, 0], sibling
-        )
+            came = s2_recv[j].astype(F32)
+            for half in range(2):
+                k = 2 * j + half
+                mixed = acc[k] + came[half * part_rows : (half + 1) * part_rows]
+                square = square + jnp.sum(mixed * mixed, axis=1, keepdims=True)
+                fs = pl.ds(pl.multiple_of(core * wing + k * chunk, HEAD), chunk)
+                part = part + dot((mixed * out_gain[:, fs]).astype(BF16), w_f[fs, :])
+        channels = part.shape[1]
+        vel_send[...] = jnp.concatenate(
+            [part, jnp.broadcast_to(square, (part_rows, HEAD))], axis=1
+        )
+        near = tile_copy(vel_send, vel_recv, v_ss.at[step, 0], v_rs.at[step, 0], sibling)
         near.start()
         near.wait_recv()
-        both = vel_send[0] + vel_recv[0]
-        vel_send[1] = both
-        others = []
-        for j in range(1, ny):
-            copy = tile_copy(
-                vel_send.at[1],
-                vel_recv.at[j],
-                v_ss.at[step, j],
-                v_rs.at[step, j],
-                lax.rem(ty + j, ny) * 2 + core,
-            )
-            copy.start()
-            others.append(copy)
-        for j, copy in enumerate(others):
-            copy.wait_recv()
-            both = both + vel_recv[j + 1]
-        channels = part.shape[1]
+        both = vel_send[...] + vel_recv[...]
         scale = lax.rsqrt(both[:, channels : channels + 1] / width + EPSILON)
-        new_state = state - step_sizes[step] * (both[:, :channels] * scale)
-        state_out[...] = new_state
+        fresh = state_ref[near_rows, :] - step_sizes[step] * (both[:, :channels] * scale)
+        st_send[...] = fresh
+        over = tile_copy(st_send, st_recv.at[step], v_ss.at[step, 1], v_rs.at[step, 1], across)
+        over.start()
+        over.wait_recv()
+        other = st_recv[step]
+        new_state = jnp.concatenate(
+            [jnp.where(ty == 0, fresh, other), jnp.where(ty == 0, other, fresh)], axis=0
+        )
+        state_ref[...] = new_state
         if step < STEPS - 1:
-            p_send[...] = padded(new_state).astype(BF16)
+            p_send[...] = new_state.astype(BF16)
             remote(p_send, p_recv, p_ss, p_rs, mate).start()
-        for _, copy in first:
+        for copy in first + second + [near, over] + swaps:
             copy.wait_send()
-        for _, copy in second:
-            copy.wait_send()
-        near.wait_send()
-        for copy in others:
-            copy.wait_send()
-        for copy in swaps:
-            copy.wait_send()
-
-    vid[me] = state_out[:VID_DEV, :].astype(BF16)
+
+    mine = dot(sel[...].reshape(n * sent, VID_DEV), state_ref[0:VID_DEV, :].astype(BF16))
+    vid[...] = mine.astype(BF16).reshape(n, sent, HEAD)
     sends = []
-    for j in list(range(1, n)):
-        copy = remote(vid.at[me], vid.at[me], vid_ss.at[j], vid_rs.at[j], lax.rem(me + j, n))
+    for j in range(1, n):
+        copy = remote(
+            vid.at[j], got.at[me, 0:sent], vid_ss.at[j], vid_rs.at[j], lax.rem(me + j, n)
+        )
         copy.start()
         sends.append(copy)
+    got[me, 0:sent] = vid[0]
+    state_out[...] = state_ref[0:rows, :]
 
     remote(p_send, p_recv, p_ss, p_rs, mate).wait_send()
     for di in range(2):
@@ -653,8 +707,9 @@
     need(7)
     for j in range(1, n):
         source = lax.rem(me - j + n, n)
-        remote(vid.at[source], vid.at[source], vid_ss.at[j], vid_rs.at[j], source).wait_recv()
-    grown[...] = dot(onehot[...], vid[...].reshape(n * VID_DEV, HEAD))
+        landed = got.at[source, 0:sent]
+        remote(vid.at[j], landed, vid_ss.at[j], vid_rs.at[j], source).wait_recv()
+    grown[...] = dot(place[...], got[...].reshape(n * room, HEAD))
     pieces = []
     for a in range(3):
         for b in range(3):
@@ -700,14 +755,18 @@
     width = w_query.shape[0]
     cols = w_query.shape[1]
     pad = -(-rows // 16) * 16
-    quarter = width // nt
-    ny = nt // 2
+    part_rows = pad // (nt // 2)
+    wing = width // 2
+    chunk = 256
+    chunks = wing // chunk
     nz = n // 2
     hw = cols // 2
     nh = hw // HEAD
     bw = VID_DEV // (nt * FRAMES * BH)
     border = (BH + 2) * (bw + 2) * 2 * FRAMES
     cells = FRAMES * BH * bw
+    sent = -(-9 * VID_DEV // (n * nt * 16)) * 16
+    room = next(r for r in (16, 32, 64, 128) if r >= sent)
     out_ch = conv_w.shape[-1]
     conv_flat = conv_w.reshape(-1, out_ch)
     vmem = pl.BlockSpec(memory_space=pltpu.VMEM)
@@ -728,12 +787,12 @@
             pltpu.VMEM(w_out.shape, BF16),
             pltpu.VMEM(w_final.shape, BF16),
             pltpu.VMEM(conv_flat.shape, BF16),
-            pltpu.VMEM((n + 2 + nz, nh, 2, pad, HEAD), BF16),
-            pltpu.VMEM((n + 2, nh, 2, pad, HEAD), BF16),
+            pltpu.VMEM((n + 2 + nz, nh, 2 * rows, HEAD), BF16),
+            pltpu.VMEM((n + 2, nh, 2 * rows, HEAD), BF16),
             pltpu.VMEM((2, nz, pad, HEAD), BF16),
             pltpu.VMEM((2 * rows, width), F32),
             pltpu.VMEM((2 * rows, width), BF16),
-            pltpu.VMEM((pad, quarter), F32),
+            pltpu.VMEM((pad, wing), F32),
             pltpu.VMEM((2, nh, pad, HEAD), BF16),
             pltpu.VMEM((2, 2, rows, HEAD), F32),
             pltpu.VMEM((2, 2 * rows, HEAD), F32),
@@ -742,15 +801,20 @@
             pltpu.VMEM((STEPS, nh, pad, HEAD), BF16),
             pltpu.VMEM((pad, HEAD), BF16),
             pltpu.VMEM((pad, HEAD), BF16),
-            pltpu.VMEM((pad, quarter), F32),
-            pltpu.VMEM((ny, pad, quarter), BF16),
-            pltpu.VMEM((ny, pad, quarter), BF16),
-            pltpu.VMEM((ny - 1, pad, quarter), BF16),
-            pltpu.VMEM((ny - 1, pad, quarter), BF16),
-            pltpu.VMEM((2, rows, channels + HEAD), F32),
-            pltpu.VMEM((ny, rows, channels + HEAD), F32),
-            pltpu.VMEM((n, VID_DEV, channels), BF16),
-            pltpu.VMEM((border, n * VID_DEV), BF16),
+            pltpu.VMEM((pad, channels), F32),
+            pltpu.VMEM((part_rows, channels), F32),
+            pltpu.VMEM((STEPS, part_rows, channels), F32),
+            pltpu.VMEM((chunks, part_rows, chunk), F32),
+            pltpu.VMEM((chunks, pad, chunk), BF16),
+            pltpu.VMEM((chunks, pad, chunk), BF16),
+            pltpu.VMEM((chunks // 2, pad, chunk), BF16),
+            pltpu.VMEM((chunks // 2, pad, chunk), BF16),
+            pltpu.VMEM((part_rows, channels + HEAD), F32),
+            pltpu.VMEM((part_rows, channels + HEAD), F32),
+            pltpu.VMEM((n, sent, channels), BF16),
+            pltpu.VMEM((n, room, channels), BF16),
+            pltpu.VMEM((n, sent, VID_DEV), BF16),
+            pltpu.VMEM((border, n * room), BF16),
             pltpu.VMEM((border, channels), F32),
             dma((8,)),
             dma((2, nz - 1)),
@@ -765,12 +829,12 @@
             dma((STEPS, nh)),
             dma(()),
             dma(()),
-            dma((STEPS, ny)),
-            dma((STEPS, ny)),
-            dma((STEPS, ny)),
-            dma((STEPS, ny)),
-            dma((STEPS, ny)),
-            dma((STEPS, ny)),
+            dma((STEPS, chunks)),
+            dma((STEPS, chunks)),
+            dma((STEPS, chunks // 2)),
+            dma((STEPS, chunks // 2)),
+            dma((STEPS, 2)),
+            dma((STEPS, 2)),
             dma((n,)),
             dma((n,)),
         ],

time: 89.4 us -> 81.4 us (0.911)
  Pallas kernels: 85.6 us -> 77.6 us
    pallas_call x1, Pallas kernels: 85.6 us -> 77.6 us  [local(): pl.pallas_call(functools.partial(kernel, n, nt), out_shape=(jax.ShapeDtyp...]
where the time goes in v2:
time: 81.4 us; the launch traced here: 81.2 us
  Pallas kernels  77.6 us (95%)
  local copies, waits for them, and re-layouts  2.92 us (4%)
    pallas_call x1, Pallas kernels, local(): pl.pallas_call(functools.partial(kernel, n, nt), out_shape=(jax.ShapeDtyp...  77.6 us

profile of v2, /device:TPU:0, one launch (start us, length us, event | category | flops | bytes accessed | tf_op | source)
XLA Modules:
  0.0 81.2 jit_solution(342865154826209268)
XLA Ops:
  0.6 77.6 %shard_map.203 = (f32[136,128]{1,0:T(8,128)}, bf16[32,512]{1,0:T(8,128)(2,1)}) custom-call(f32[136,128]{1,0:T(8,128)} %latents.1, s32[1,136]{1,0:T(1,128)} %bitcast.19, s32[1,1024]{1,0:T(1,128)} %bitcast.15, f32[2,3072]{1,0:T(2,128)} %mod_scale.1, f32[2,3072]{1,0:T(2,128)} %mod_shift.1, f32[6,128]{1,0:T(8,128)} %bitcast.16, f32[6,128]{1,0:T(8,128)} %bitcast.17, ...), custom_call_target="tpu_custom_call" | custom-call | tf_op jit(solution)/shard_map/pallas_call | solution.py:775
  78.2 1.4 %copy.24 = bf16[2,2,8,512]{3,1,0,2:T(2,128)(2,1)} copy(bf16[2,2,8,512]{3,2,1,0:T(8,128)(2,1)} %bitcast.13) | data formatting | bytes 65536 | tf_op jit(solution)/shard_map/reshape | solution.py:866
  79.6 1.5 %copy.26 = f32[136,128]{1,0:T(8,128)} copy(f32[136,128]{1,0:T(8,128)} %get-tuple-element.8) | data formatting | bytes 139264

commit v3 on v2

--- a/solution.py
+++ b/solution.py
@@ -147,14 +147,18 @@
 
     got[...] = jnp.zeros(got.shape, BF16)
     barrier = pltpu.get_barrier_semaphore()
-    for j in range(1, n):
-        pl.semaphore_signal(
-            barrier, inc=1, device_id=(lax.rem(me + j, n), tile), device_id_type=MESH
-        )
-    for j in range(1, nt):
-        pl.semaphore_signal(
-            barrier, inc=1, device_id=(me, lax.rem(tile + j, nt)), device_id_type=MESH
-        )
+    for z, z_there in ((-1, zz > 0), (1, zz < nz - 1)):
+
+        @pl.when(z_there)
+        def _():
+            pl.semaphore_signal(
+                barrier, inc=1, device_id=(me + 2 * z, tile), device_id_type=MESH
+            )
+
+    sibling = ty * 2 + 1 - core
+    across = (1 - ty) * 2 + core
+    for spot in ((me + 1 - 2 * xx, tile), (me, sibling), (me, across)):
+        pl.semaphore_signal(barrier, inc=1, device_id=spot, device_id_type=MESH)
 
     def padded(x):
         return jnp.concatenate([x, jnp.zeros((pad - rows, x.shape[1]), F32)], axis=0)
@@ -177,7 +181,7 @@
         for a, slot in ((h, 1), (1 - h, n + 2 + zz)):
             cs = pl.ds(pl.multiple_of(a * hw + i * HEAD, HEAD), HEAD)
             put_kv(kv0, slot, i, k_cache[:, cs].astype(F32), v_cache[:, cs].astype(F32))
-    pl.semaphore_wait(barrier, n - 1 + nt - 1)
+    pl.semaphore_wait(barrier, 5 - jnp.where((zz == 0) | (zz == nz - 1), 1, 0))
 
     def remote(src, dst, ss, rs, patch):
         return pltpu.make_async_remote_copy(
@@ -517,6 +521,11 @@
         project_kv(2, pair_cs[0], pair_cs[1], put)
         for e in range(each // 2, each):
             event(base + e)
+
+    for j in range(1, n):
+        pl.semaphore_signal(
+            barrier, inc=1, device_id=(lax.rem(me + j, n), tile), device_id_type=MESH
+        )
 
     def attend(keys_of, r, first, i):
         span = slice(first, first + n)
@@ -603,8 +612,6 @@
                 device_id_type=MESH,
             )
 
-        sibling = ty * 2 + 1 - core
-        across = (1 - ty) * 2 + core
         near_rows = pl.ds(pl.multiple_of(ty * part_rows, 8), part_rows)
         first = []
         for k in range(chunks):
@@ -672,6 +679,7 @@
     mine = dot(sel[...].reshape(n * sent, VID_DEV), state_ref[0:VID_DEV, :].astype(BF16))
     vid[...] = mine.astype(BF16).reshape(n, sent, HEAD)
     sends = []
+    pl.semaphore_wait(barrier, n - 1)
     for j in range(1, n):
         copy = remote(
             vid.at[j], got.at[me, 0:sent], vid_ss.at[j], vid_rs.at[j], lax.rem(me + j, n)
@@ -723,9 +731,18 @@
                     jnp.concatenate([grown[s : s + FRAMES, :] for s in starts], axis=0).astype(BF16)
                 )
     total = dot(jnp.concatenate(pieces, axis=1), w_c[...])
-    conv_out[...] = (total + conv_b[...]).astype(BF16)
+    conv_out[...] = total + conv_b[...]
     for copy in sends:
         copy.wait_send()
+
+
+def finish(state, conv, state_out, decoded):
+    state_out[...] = state[...]
+    bw = decoded.shape[2]
+    for h in range(BH):
+        for w in range(bw):
+            first = (h * bw + w) * FRAMES
+            decoded[:, h, w, :] = conv[first : first + FRAMES, :].astype(BF16)
 
 
 def local(
@@ -776,7 +793,7 @@
         functools.partial(kernel, n, nt),
         out_shape=(
             jax.ShapeDtypeStruct((rows, channels), F32),
-            jax.ShapeDtypeStruct((cells, out_ch), BF16),
+            jax.ShapeDtypeStruct((cells, out_ch), F32),
         ),
         in_specs=[vmem] * 10 + [pl.BlockSpec(memory_space=pltpu.SMEM), vmem] + [hbm] * 8,
         out_specs=(vmem, vmem),
@@ -863,8 +880,15 @@
         w_final,
         conv_flat,
     )
-    decoded = conv.reshape(BH, bw, FRAMES, out_ch).transpose(2, 0, 1, 3)
-    return state, decoded
+    return pl.pallas_call(
+        finish,
+        out_shape=(
+            jax.ShapeDtypeStruct((rows, channels), F32),
+            jax.ShapeDtypeStruct((FRAMES, BH, bw, out_ch), BF16),
+        ),
+        in_specs=[vmem, vmem],
+        out_specs=(vmem, vmem),
+    )(state, conv)
 
 
 def solution(mesh):

time: 81.4 us -> 79 us (0.971)
  local copies, waits for them, and re-layouts: 2.92 us -> 0 us
    pallas_call x0 -> x1, Pallas kernels: none -> 1.53 us  [local(): pl.pallas_call(finish, out_shape=(jax.ShapeDtypeStruct((rows, channels),...]
    unnamed x1 -> x0, local copies, waits for them, and re-layouts: 1.52 us -> none
    reshape x1 -> x0, local copies, waits for them, and re-layouts: 1.4 us -> none  [local(): decoded = conv.reshape(BH, bw, FRAMES, out_ch).transpose(2, 0, 1, 3)]
    pallas_call x1, Pallas kernels: 77.6 us -> 76.6 us  [local(): pl.pallas_call(functools.partial(kernel, n, nt), out_shape=(jax.ShapeDtyp...]
where the time goes in v3:
time: 79 us; the launch traced here: 78.8 us
  Pallas kernels  78.1 us (99%)
    pallas_call x1, Pallas kernels, local(): pl.pallas_call(functools.partial(kernel, n, nt), out_shape=(jax.ShapeDtyp...  76.6 us

profile of v3, /device:TPU:0, one launch (start us, length us, event | category | flops | bytes accessed | tf_op | source)
XLA Modules:
  0.0 78.8 jit_solution(14523705510667625820)
XLA Ops:
  0.6 76.6 %shard_map.203 = (f32[136,128]{1,0:T(8,128)}, f32[32,512]{1,0:T(8,128)}) custom-call(f32[136,128]{1,0:T(8,128)} %latents.1, s32[1,136]{1,0:T(1,128)} %bitcast.13, s32[1,1024]{1,0:T(1,128)} %bitcast.9, f32[2,3072]{1,0:T(2,128)} %mod_scale.1, f32[2,3072]{1,0:T(2,128)} %mod_shift.1, f32[6,128]{1,0:T(8,128)} %bitcast.10, f32[6,128]{1,0:T(8,128)} %bitcast.11, ...), custom_call_target="tpu_custom_call" | custom-call | tf_op jit(solution)/shard_map/pallas_call | solution.py:792
  77.2 1.5 %shard_map.204 = (f32[136,128]{1,0:T(8,128)}, bf16[8,2,2,512]{3,2,1,0:T(2,128)(2,1)}) custom-call(f32[136,128]{1,0:T(8,128)} %get-tuple-element.4.state, f32[32,512]{1,0:T(8,128)} %get-tuple-element.5.conv), custom_call_target="tpu_custom_call" | custom-call | tf_op jit(solution)/shard_map/pallas_call | solution.py:883

commit v4 on v3

--- a/solution.py
+++ b/solution.py
@@ -1,4 +1,5 @@
 import functools
+import math
 
 import jax
 import jax.numpy as jnp
@@ -14,6 +15,7 @@
 FRAMES = 8
 BH = 2
 EPSILON = 1e-06
+SCALE = HEAD ** (-0.5) * math.log2(math.e)
 MESH = pl.DeviceIdType.MESH
 F32 = jnp.float32
 BF16 = jnp.bfloat16
@@ -53,21 +55,17 @@
     w_qkv,
     w_o,
     w_f,
-    w_c,
     kv0,
     kv1,
     lat,
     emb,
     normed,
-    embq,
     q_ref,
     cs_ref,
     pair_cs,
     table,
     att,
     o_send,
-    p_send,
-    p_recv,
     state_ref,
     st_send,
     st_recv,
@@ -94,8 +92,6 @@
     kx_rs,
     o_ss,
     o_rs,
-    p_ss,
-    p_rs,
     s1_ss,
     s1_rs,
     s2_ss,
@@ -108,10 +104,11 @@
     rows = latents.shape[0]
     pad = lat.shape[2]
     width = emb.shape[1]
-    hw = w_qkv.shape[1] // 3
+    hw = w_qkv.shape[1] // 6
     nh = hw // HEAD
     part_rows = pad // (nt // 2)
     wing = width // 2
+    taps, out_ch = cw_hbm.shape
     nz = n // 2
     npz = nz // 2
     me = lax.axis_index("patch")
@@ -138,12 +135,16 @@
             (wq_hbm.at[:, half_cols(h)], w_qkv.at[:, 2 * hw : 3 * hw]),
             (wo_hbm, w_o),
             (wf_hbm, w_f),
-            (cw_hbm, w_c),
+            (cw_hbm.at[0:width], w_qkv.at[:, 0:out_ch]),
+            (cw_hbm.at[width:taps], w_qkv.at[0 : taps - width, out_ch : 2 * out_ch]),
+            (wk_hbm.at[:, half_cols(1 - h)], w_qkv.at[:, 3 * hw : 4 * hw]),
+            (wval_hbm.at[:, half_cols(1 - h)], w_qkv.at[:, 4 * hw : 5 * hw]),
+            (wq_hbm.at[:, half_cols(1 - h)], w_qkv.at[:, 5 * hw : 6 * hw]),
         )
     ):
-        copy = pltpu.make_async_copy(src, dst, load_sem.at[i])
-        copy.start()
-        loads.append(copy)
+        loads.append(pltpu.make_async_copy(src, dst, load_sem.at[i]))
+    for i in (0, 1, 2, 3, 4, 9, 10, 11, 5, 6):
+        loads[i].start()
 
     got[...] = jnp.zeros(got.shape, BF16)
     barrier = pltpu.get_barrier_semaphore()
@@ -360,21 +361,22 @@
         x = x * gain
         return x * cos + pltpu.roll(x, HEAD // 2, 1) * sin
 
-    def gain_row(gain, i):
-        return gain[pl.ds(h * nh + i, 1), :]
-
-    def project_kv(count, cos, sin, put):
-        raw = dot(normed[0 : count * rows, :], w_qkv[:, 0 : 2 * hw])
+    def gain_row(gain, a, i):
+        return gain[pl.ds((h if a == 0 else 1 - h) * nh + i, 1), :]
+
+    def project_kv(count, a, cos, sin, put):
+        raw = dot(normed[0 : count * rows, :], w_qkv[:, 3 * a * hw : (3 * a + 2) * hw])
         for i in range(nh):
-            k = rotate(raw[:, i * HEAD : (i + 1) * HEAD], gain_row(k_gain, i), cos, sin)
+            k = rotate(raw[:, i * HEAD : (i + 1) * HEAD], gain_row(k_gain, a, i), cos, sin)
             v = raw[:, hw + i * HEAD : hw + (i + 1) * HEAD]
             for g in range(count):
-                put(g, i, shard_rows(k, g, count), shard_rows(v, g, count))
-
-    def project_q(count, cos, sin, targets):
-        raw = dot(normed[0 : count * rows, :], w_qkv[:, 2 * hw : 3 * hw])
+                put(g, a, i, shard_rows(k, g, count), shard_rows(v, g, count))
+
+    def project_q(count, a, cos, sin, targets):
+        raw = dot(normed[0 : count * rows, :], w_qkv[:, (3 * a + 2) * hw : 3 * (a + 1) * hw])
         for i in range(nh):
-            q = rotate(raw[:, i * HEAD : (i + 1) * HEAD], gain_row(q_gain, i), cos, sin)
+            gain = gain_row(q_gain, a, i) * SCALE
+            q = rotate(raw[:, i * HEAD : (i + 1) * HEAD], gain, cos, sin)
             for g in range(count):
                 q_ref[targets[g], i] = padded(shard_rows(q, g, count)).astype(BF16)
 
@@ -402,35 +404,44 @@
         kv_cross(zz, i, 1).start()
 
     own_blocks = [lat[xx, zz].astype(F32), lat[xx, zz + 1 - 2 * h].astype(F32)]
-    es = pl.ds(pl.multiple_of(core * wing, HEAD), wing)
     need(0)
     need(1)
     embed(own_blocks, 0)
-    embq[...] = padded(
-        jnp.concatenate(
-            [emb[0:VID_DEV, es], emb[2 * VID_DEV : 2 * VID_DEV + AUD_DEV, es]], axis=0
-        )
-    )
+
+    def keep_near(count):
+        for k in range(chunks):
+            es = pl.ds(pl.multiple_of(core * wing + k * chunk, HEAD), chunk)
+            last = emb[count * VID_DEV : count * VID_DEV + AUD_DEV, es]
+            full = padded(jnp.concatenate([emb[0:VID_DEV, es], last], axis=0))
+            acc[k] = jnp.where(ty == 0, full[:part_rows], full[part_rows:])
+
+    keep_near(2)
     if nz > 2:
         lat_event(2)
     start_own(1, range(nh))
     pair_waves(own_blocks)
-    for g in range(2):
-        for k in range(2):
-            cs_ref[g, k] = shard_rows(pair_cs[k], g, 2)
-
-    def put_own(g, i, k, v):
-        put_kv(kv0, n + 1 if g == 0 else 0, i, k, v)
-        put_kv(kv1, 1 if g == 0 else n, i, k, v)
+    for k in range(2):
+        cs_ref[k] = shard_rows(pair_cs[k], 0, 2)
+
+    def put_own(g, a, i, k, v):
+        if a == 0:
+            put_kv(kv0, n + 1 if g == 0 else 0, i, k, v)
+        if g == 1:
+            put_kv(kv1.at[a], 0, i, k, v)
 
     need(2)
     need(3)
-    project_kv(2, pair_cs[0], pair_cs[1], put_own)
+    project_kv(2, 0, pair_cs[0], pair_cs[1], put_own)
     for d in range(3, nz):
         lat_event(d)
     need(4)
-    project_q(2, pair_cs[0], pair_cs[1], (0, 1))
+    project_q(2, 0, pair_cs[0], pair_cs[1], (0, 1))
     for e in range(nh):
+        event(e)
+    need(9)
+    need(10)
+    project_kv(2, 1, pair_cs[0], pair_cs[1], put_own)
+    for e in range(nh, 2 * nh):
         event(e)
 
     bw = VID_DEV // (nt * FRAMES * BH)
@@ -493,14 +504,27 @@
 
     pairs = n // 2
     total_events = (nz - 1) * 2 * nh
-    each = -(-(total_events - nh) // (pairs - 1))
-
-    @pl.loop(1, pairs)
-    def _(j):
+    each = -(-(total_events - 2 * nh) // (pairs - 1))
+    marks = [each * k // 3 for k in range(4)]
+
+    early = pairs // 4
+
+    def pair_of(j):
         line = j % 2
         turn = j // 2
         first = 2 * lax.rem(zz // 2 + turn, npz)
         side = jnp.where(line == 0, xx, 1 - xx)
+        return line, first, side, jnp.where(line == 1, nz + first, 2 * turn)
+
+    def put_at(slot):
+        def put(g, a, i, k, v):
+            put_kv(kv1.at[a], slot + g, i, k, v)
+
+        return put
+
+    @pl.loop(1, pairs)
+    def _(j):
+        line, first, side, slot = pair_of(j)
 
         @pl.when(line == 1)
         def _():
@@ -509,25 +533,36 @@
 
         blocks = [lat[side, first + g].astype(F32) for g in range(2)]
         embed(blocks, 0)
-        base = nh + (j - 1) * each
-        for e in range(each // 2):
+        base = 2 * nh + (j - 1) * each
+        for e in range(marks[0], marks[1]):
             event(base + e)
         pair_waves(blocks)
-        slot = jnp.where(line == 1, nz + first, 2 * turn)
-
-        def put(g, i, k, v):
-            put_kv(kv1, slot + g, i, k, v)
-
-        project_kv(2, pair_cs[0], pair_cs[1], put)
-        for e in range(each // 2, each):
+        project_kv(2, 0, pair_cs[0], pair_cs[1], put_at(slot))
+        for e in range(marks[1], marks[2]):
             event(base + e)
+
+        @pl.when(j <= early)
+        def _():
+            project_kv(2, 1, pair_cs[0], pair_cs[1], put_at(slot))
+
+        for e in range(marks[2], marks[3]):
+            event(base + e)
+
+    def late_pairs():
+        @pl.loop(early + 1, pairs)
+        def _(j):
+            line, first, side, slot = pair_of(j)
+            blocks = [lat[side, first + g].astype(F32) for g in range(2)]
+            embed(blocks, 0)
+            pair_waves(blocks)
+            project_kv(2, 1, pair_cs[0], pair_cs[1], put_at(slot))
 
     for j in range(1, n):
         pl.semaphore_signal(
             barrier, inc=1, device_id=(lax.rem(me + j, n), tile), device_id_type=MESH
         )
 
-    def attend(keys_of, r, first, i):
+    def score(keys_of, r, first, i):
         span = slice(first, first + n)
         last = keys_of[span, i, 2 * VID_DEV : 2 * rows].astype(F32)
         last_keys = last[:, :AUD_DEV].reshape(n * AUD_DEV, HEAD).astype(BF16)
@@ -542,58 +577,56 @@
         scores = lax.dot_general(
             q_ref[r, i], keys, (((1,), (1,)), ((), ())), preferred_element_type=F32
         )
-        top = jnp.max(scores, axis=1, keepdims=True)
-        weights = jnp.exp((scores - top) * HEAD ** (-0.5))
+        return scores, jnp.max(scores, axis=1, keepdims=True), values
+
+    def attend(held):
+        scores, top, values = held
+        weights = jnp.exp2(scores - top)
         total = jnp.sum(weights, axis=1, keepdims=True)
         return (dot(weights.astype(BF16), values) / total).astype(BF16)
 
+    batch = nh if n * rows <= 2048 else 1
+
+    def attend_all(keys_of, r, first, result):
+        for k in range(0, nh, batch):
+            held = [score(keys_of, r, first, i) for i in range(k, min(k + batch, nh))]
+            for i, parts in enumerate(held):
+                result[k + i] = attend(parts)
+
     for step in range(STEPS):
         state = state_ref[...]
-        if step > 0:
-
-            def put_fresh(g, i, k, v):
-                put_kv(kv1, n + 1, i, k, v)
-
-            def put_mate(g, i, k, v):
-                put_kv(kv1, 0, i, k, v)
-
-            embed([state], step)
-            embq[...] = padded(emb[0:rows, es])
-            project_kv(1, cs_ref[0, 0], cs_ref[0, 1], put_fresh)
-            project_q(1, cs_ref[0, 0], cs_ref[0, 1], (0,))
-            remote(p_send, p_recv, p_ss, p_rs, mate).wait_recv()
-            embed([p_recv[...].astype(F32)], step)
-            project_kv(1, cs_ref[1, 0], cs_ref[1, 1], put_mate)
-            project_q(1, cs_ref[1, 0], cs_ref[1, 1], (1,))
-        keys_of = kv0 if step == 0 else kv1
-        swaps = []
-        for i in range(nh):
-            if step == 0:
+        if step == 0:
+            swaps = []
+            for i in range(nh):
                 for s in range(nz):
                     kv_cross(s, i, nz + s).wait_recv()
-            o_send[step, i] = attend(keys_of, 1, 0, i)
-            copy = remote(
-                o_send.at[step, i],
-                att.at[step, h, i],
-                o_ss.at[step, i],
-                o_rs.at[step, i],
-                mate,
-            )
-            copy.start()
-            swaps.append(copy)
-        for i in range(nh):
-            att[step, h, i] = attend(keys_of, 0, 2, i)
-        need(5)
-        for i in range(nh):
-            remote(
-                o_send.at[step, i],
-                att.at[step, 1 - h, i],
-                o_ss.at[step, i],
-                o_rs.at[step, i],
-                mate,
-            ).wait_recv()
-
-        heads = [att[step, a, i] for a in range(2) for i in range(nh)]
+                o_send[i] = attend(score(kv0, 1, 0, i))
+                copy = remote(o_send.at[i], att.at[h, i], o_ss.at[i], o_rs.at[i], mate)
+                copy.start()
+                swaps.append(copy)
+            attend_all(kv0, 0, 2, att.at[h])
+            need(5)
+            for i in range(nh):
+                remote(
+                    o_send.at[i], att.at[1 - h, i], o_ss.at[i], o_rs.at[i], mate
+                ).wait_recv()
+        else:
+
+            def put_fresh(g, a, i, k, v):
+                put_kv(kv1.at[a], 1, i, k, v)
+
+            embed([state], step)
+            keep_near(1)
+            need(11)
+            for a in range(2):
+                project_kv(1, a, cs_ref[0], cs_ref[1], put_fresh)
+                project_q(1, a, cs_ref[0], cs_ref[1], (a,))
+            for i in (7, 8):
+                loads[i].start()
+            for a in range(2):
+                attend_all(kv1.at[a], a, 0, att.at[h if a == 0 else 1 - h])
+
+        heads = [att[a, i] for a in range(2) for i in range(nh)]
         whole = jnp.concatenate(heads, axis=1).astype(F32)
         turned = jnp.concatenate([whole[part_rows:], whole[:part_rows]], axis=0)
         mine_att = jnp.where(ty == 0, turned, whole).astype(BF16)
@@ -628,8 +661,7 @@
             first[k].wait_recv()
             mine = mine + s1_recv[k].astype(F32)
             far_parts.append(mine[:part_rows])
-            ks = pl.ds(k * chunk, chunk)
-            acc[k] = mine[part_rows:] + embq[near_rows, ks]
+            acc[k] += mine[part_rows:]
             if k % 2 == 1:
                 j = k // 2
                 s2_send[j] = jnp.concatenate(far_parts, axis=0).astype(BF16)
@@ -639,6 +671,8 @@
                 )
                 far.start()
                 second.append(far)
+        if step == 0:
+            late_pairs()
         need(6)
         square = jnp.zeros((part_rows, 1), F32)
         part = jnp.zeros((part_rows, w_f.shape[1]), F32)
@@ -670,10 +704,7 @@
             [jnp.where(ty == 0, fresh, other), jnp.where(ty == 0, other, fresh)], axis=0
         )
         state_ref[...] = new_state
-        if step < STEPS - 1:
-            p_send[...] = new_state.astype(BF16)
-            remote(p_send, p_recv, p_ss, p_rs, mate).start()
-        for copy in first + second + [near, over] + swaps:
+        for copy in first + second + [near, over] + (swaps if step == 0 else []):
             copy.wait_send()
 
     mine = dot(sel[...].reshape(n * sent, VID_DEV), state_ref[0:VID_DEV, :].astype(BF16))
@@ -689,7 +720,6 @@
     got[me, 0:sent] = vid[0]
     state_out[...] = state_ref[0:rows, :]
 
-    remote(p_send, p_recv, p_ss, p_rs, mate).wait_send()
     for di in range(2):
         for d in range(1, nz):
             go, copy = lat_send(di, d)
@@ -713,6 +743,7 @@
                 copy.wait_send()
 
     need(7)
+    need(8)
     for j in range(1, n):
         source = lax.rem(me - j + n, n)
         landed = got.at[source, 0:sent]
@@ -730,7 +761,10 @@
                 pieces.append(
                     jnp.concatenate([grown[s : s + FRAMES, :] for s in starts], axis=0).astype(BF16)
                 )
-    total = dot(jnp.concatenate(pieces, axis=1), w_c[...])
+    cut = width // HEAD
+    total = dot(jnp.concatenate(pieces[:cut], axis=1), w_qkv[:, 0:out_ch])
+    rest = w_qkv[0 : taps - width, out_ch : 2 * out_ch]
+    total = total + dot(jnp.concatenate(pieces[cut:], axis=1), rest)
     conv_out[...] = total + conv_b[...]
     for copy in sends:
         copy.wait_send()
@@ -800,24 +834,20 @@
         scratch_shapes=[
             pltpu.VMEM(w_video.shape, BF16),
             pltpu.VMEM(w_audio.shape, BF16),
-            pltpu.VMEM((width, 3 * hw), BF16),
+            pltpu.VMEM((width, 6 * hw), BF16),
             pltpu.VMEM(w_out.shape, BF16),
             pltpu.VMEM(w_final.shape, BF16),
-            pltpu.VMEM(conv_flat.shape, BF16),
             pltpu.VMEM((n + 2 + nz, nh, 2 * rows, HEAD), BF16),
-            pltpu.VMEM((n + 2, nh, 2 * rows, HEAD), BF16),
+            pltpu.VMEM((2, n, nh, 2 * rows, HEAD), BF16),
             pltpu.VMEM((2, nz, pad, HEAD), BF16),
             pltpu.VMEM((2 * rows, width), F32),
             pltpu.VMEM((2 * rows, width), BF16),
-            pltpu.VMEM((pad, wing), F32),
             pltpu.VMEM((2, nh, pad, HEAD), BF16),
-            pltpu.VMEM((2, 2, rows, HEAD), F32),
+            pltpu.VMEM((2, rows, HEAD), F32),
             pltpu.VMEM((2, 2 * rows, HEAD), F32),
             pltpu.VMEM((HEAD, 2 * HEAD), BF16),
-            pltpu.VMEM((STEPS, 2, nh, pad, HEAD), BF16),
-            pltpu.VMEM((STEPS, nh, pad, HEAD), BF16),
-            pltpu.VMEM((pad, HEAD), BF16),
-            pltpu.VMEM((pad, HEAD), BF16),
+            pltpu.VMEM((2, nh, pad, HEAD), BF16),
+            pltpu.VMEM((nh, pad, HEAD), BF16),
             pltpu.VMEM((pad, channels), F32),
             pltpu.VMEM((part_rows, channels), F32),
             pltpu.VMEM((STEPS, part_rows, channels), F32),
@@ -833,7 +863,7 @@
             pltpu.VMEM((n, sent, VID_DEV), BF16),
             pltpu.VMEM((border, n * room), BF16),
             pltpu.VMEM((border, channels), F32),
-            dma((8,)),
+            dma((12,)),
             dma((2, nz - 1)),
             dma((2, nz - 1)),
             dma((nz,)),
@@ -842,10 +872,8 @@
             dma((2, nz - 1, 2, nh)),
             dma((nz, nh)),
             dma((nz, nh)),
-            dma((STEPS, nh)),
-            dma((STEPS, nh)),
-            dma(()),
-            dma(()),
+            dma((nh,)),
+            dma((nh,)),
             dma((STEPS, chunks)),
             dma((STEPS, chunks)),
             dma((STEPS, chunks // 2)),

time: 79 us -> 76.6 us (0.970)
  Pallas kernels: 78.1 us -> 75.7 us
    pallas_call x1, Pallas kernels: 76.6 us -> 74.2 us  [local(): pl.pallas_call(functools.partial(kernel, n, nt), out_shape=(jax.ShapeDtyp...]
where the time goes in v4:
time: 76.6 us; the launch traced here: 76.4 us
  Pallas kernels  75.7 us (99%)
    pallas_call x1, Pallas kernels, local(): pl.pallas_call(functools.partial(kernel, n, nt), out_shape=(jax.ShapeDtyp...  74.2 us
    pallas_call x1, Pallas kernels, local(): pl.pallas_call(finish, out_shape=(jax.ShapeDtypeStruct((rows, channels),...  1.53 us

profile of v4, /device:TPU:0, one launch (start us, length us, event | category | flops | bytes accessed | tf_op | source)
XLA Modules:
  0.0 76.4 jit_solution(7899847545384974530)
XLA Ops:
  0.6 74.2 %shard_map.203 = (f32[136,128]{1,0:T(8,128)}, f32[32,512]{1,0:T(8,128)}) custom-call(f32[136,128]{1,0:T(8,128)} %latents.1, s32[1,136]{1,0:T(1,128)} %bitcast.13, s32[1,1024]{1,0:T(1,128)} %bitcast.9, f32[2,3072]{1,0:T(2,128)} %mod_scale.1, f32[2,3072]{1,0:T(2,128)} %mod_shift.1, f32[6,128]{1,0:T(8,128)} %bitcast.10, f32[6,128]{1,0:T(8,128)} %bitcast.11, ...), custom_call_target="tpu_custom_call" | custom-call | tf_op jit(solution)/shard_map/pallas_call | solution.py:826
  74.8 1.5 %shard_map.204 = (f32[136,128]{1,0:T(8,128)}, bf16[8,2,2,512]{3,2,1,0:T(2,128)(2,1)}) custom-call(f32[136,128]{1,0:T(8,128)} %get-tuple-element.4.state, f32[32,512]{1,0:T(8,128)} %get-tuple-element.5.conv), custom_call_target="tpu_custom_call" | custom-call | tf_op jit(solution)/shard_map/pallas_call | solution.py:911

commit v5 on v4

--- a/solution.py
+++ b/solution.py
@@ -440,7 +440,15 @@
         event(e)
     need(9)
     need(10)
-    project_kv(2, 1, pair_cs[0], pair_cs[1], put_own)
+    last_rows = normed[2 * VID_DEV : 2 * rows].astype(F32)[AUD_DEV:]
+    normed[0:VID_DEV] = normed[VID_DEV : 2 * VID_DEV]
+    normed[VID_DEV:rows] = last_rows.astype(BF16)
+    mate_waves = [shard_rows(pair_cs[k], 1, 2) for k in range(2)]
+
+    def put_mate(g, a, i, k, v):
+        put_kv(kv1.at[a], 0, i, k, v)
+
+    project_kv(1, 1, mate_waves[0], mate_waves[1], put_mate)
     for e in range(nh, 2 * nh):
         event(e)
 

time: 76.6 us -> 76.5 us (level)
  no operation moved by 1% of the time
where the time goes in v5:
time: 76.5 us; the launch traced here: 76.4 us
  Pallas kernels  75.7 us (99%)
    pallas_call x1, Pallas kernels, local(): pl.pallas_call(functools.partial(kernel, n, nt), out_shape=(jax.ShapeDtyp...  74.2 us
    pallas_call x1, Pallas kernels, local(): pl.pallas_call(finish, out_shape=(jax.ShapeDtypeStruct((rows, channels),...  1.53 us

profile of v5, /device:TPU:0, one launch (start us, length us, event | category | flops | bytes accessed | tf_op | source)
XLA Modules:
  0.0 76.4 jit_solution(3183428026635884419)
XLA Ops:
  0.6 74.2 %shard_map.203 = (f32[136,128]{1,0:T(8,128)}, f32[32,512]{1,0:T(8,128)}) custom-call(f32[136,128]{1,0:T(8,128)} %latents.1, s32[1,136]{1,0:T(1,128)} %bitcast.13, s32[1,1024]{1,0:T(1,128)} %bitcast.9, f32[2,3072]{1,0:T(2,128)} %mod_scale.1, f32[2,3072]{1,0:T(2,128)} %mod_shift.1, f32[6,128]{1,0:T(8,128)} %bitcast.10, f32[6,128]{1,0:T(8,128)} %bitcast.11, ...), custom_call_target="tpu_custom_call" | custom-call | tf_op jit(solution)/shard_map/pallas_call | solution.py:834
  74.8 1.5 %shard_map.204 = (f32[136,128]{1,0:T(8,128)}, bf16[8,2,2,512]{3,2,1,0:T(2,128)(2,1)}) custom-call(f32[136,128]{1,0:T(8,128)} %get-tuple-element.4.state, f32[32,512]{1,0:T(8,128)} %get-tuple-element.5.conv), custom_call_target="tpu_custom_call" | custom-call | tf_op jit(solution)/shard_map/pallas_call | solution.py:919
